TPU v7x, 32 devices: a whole 2x2x4 slice. The times are simulated.
32 devices in a mesh: chain: 4 (over y, core), col: 8 (over z, x).
Axes of the slice: x: 2, y: 2, z: 4, core: 2. Of those that a mesh axis runs over, the one named last changes fastest.
Arguments:
- sources: float32 [4, 32, 64, 128], P('chain', 'col'), may hold values from -6 to 6
- diag_inverse: float32 [4, 32, 128, 128], P('chain', 'col')
- factor_tiles: float32 [4, 752, 128, 128], P('chain', 'col'), may hold values from -0.109375 to 0.109375
- tile_rows: int32 [4, 752], P('chain', 'col'), may hold values from 0 to 31
- tile_cols: int32 [4, 752], P('chain', 'col'), may hold values from 0 to 31, as said below
Outputs:
- solved: float32 [4, 32, 64, 128], P('chain', 'col')
- leaving: float32 [4, 32, 64, 128], P('chain', 'col')
Inputs may be any that keep to these rules, and one draw needn't show every extreme that they name: `tile_cols`: entries 94 * c to 94 * (c + 1) - 1 of a group name tile columns 4 * c to 4 * (c + 1) - 1.
All inputs are finite; a program needn't handle non-finite values.
Results may differ from a plain program's by a relative error of at most 0.00018.
Values sent between devices are 32-bit elements; how exact they have to be, the bound alone decides.
A program may use at most 64 MiB of HBM per device.

v0:
```python
import jax
import jax.numpy as jnp
from jax import lax
from jax.sharding import PartitionSpec as P


def shifted(block, axis, distance):
    devices = range(lax.axis_size(axis))
    route = [(i - distance, i) for i in devices if i - distance in devices]
    return lax.ppermute(block, axis, route)


def local(sources, diag_inverse, factor_tiles, tile_rows, tile_cols):
    highest = lax.Precision.HIGHEST
    section_no = lax.axis_index("chain")
    groups = lax.axis_size("chain")
    per_device = sources.shape[1]
    source_count = sources.shape[2]
    tile_size = sources.shape[3]
    own_right = sources[0]
    inverse = diag_inverse[0]
    factor = factor_tiles[0]
    rows_index = tile_rows[0]
    local_cols = tile_cols[0] - lax.axis_index("col") * per_device
    panels = 1
    panel_width = source_count // panels
    tick_count = groups + panels - 1

    def advance(moment, state_now):
        solved, leaving, inbound = state_now
        panel_no = moment - section_no
        active = (panel_no >= 0) & (panel_no < panels)
        right_side = own_right - inbound
        current = jnp.einsum("trc,tsc->tsr", inverse, right_side, precision=highest)
        picked = jnp.take(current, local_cols, axis=0)
        products = jnp.einsum("krc,ksc->ksr", factor, picked, precision=highest)
        targets = jnp.arange(per_device * lax.axis_size("col"), dtype=jnp.int32)
        onehot = (rows_index[:, None] == targets[None, :]).astype(jnp.float32)
        shares = lax.psum_scatter(
            jnp.einsum("kt,ksr->tsr", onehot, products, precision=highest),
            "col",
            scatter_dimension=0,
            tiled=True,
        )
        received = shifted(shares, "chain", 1)
        solved = jnp.where(active, current, solved)
        leaving = jnp.where(active, shares, leaving)
        return (solved, leaving, received)

    blank = jnp.zeros((per_device, source_count, tile_size), jnp.float32)
    start_in = jnp.zeros((per_device, panel_width, tile_size), jnp.float32)
    solved, leaving, last_in = lax.fori_loop(0, tick_count, advance, (blank, blank, start_in))
    return (solved[None], leaving[None])


def solution(mesh):
    return jax.shard_map(
        local,
        mesh=mesh,
        in_specs=(
            P("chain", "col", None, None),
            P("chain", "col", None, None),
            P("chain", "col", None, None),
            P("chain", "col"),
            P("chain", "col"),
        ),
        out_specs=(P("chain", "col", None, None), P("chain", "col", None, None)),
        check_vma=False,
    )
```

profile of v0, /device:TPU:5, one launch (start us, length us, event | category | flops | bytes accessed | tf_op | source)
XLA Modules:
  0.0 376.7 jit_solution(2979506223827785505)
XLA Ops:
  7.8 361.7 %while.18 = (s32[]{:T(128)}, f32[4,64,128]{2,1,0:T(8,128)S(1)}, f32[4,64,128]{2,1,0:T(8,128)S(1)}, f32[4,64,128]{2,1,0:T(8,128)S(1)}, s32[]{:T(128)}, /*index=5*...) while((s32[]{:T(128)}, f32[4,64,128]{2,1,0:T(8,128)S(1)}, ...), condition=%wide.region_2.3_spmd.clone, body=%wide.region_0.2_spmd.clone.sunk | while | flops 1529762560 | bytes 31137972 | solution.py:52
  8.0 1.6 select_select_fusion.4
  10.3 0.7 gather_fusion
  11.0 13.7 %fusion.29 = f32[94,64,128]{2,1,0:T(8,128)S(1)} fusion(f32[94,128,128]{2,1,0:T(8,128)} %get-tuple-element.327, f32[94,64,128]{2,1,0:T(8,128)S(1)} %gather_fusion, pred[94]{0:T(512)(128)(4,1)S(1)} %compare_and_fusion.2), kind=kOutput, calls=%fused_computation.3.clone.1 | convolution fusion | flops 1183563776 | bytes 12320862 | tf_op jit(solution)/shard_map/while/body/eval_jaxpr/krc,ksc->ksr/dot_general | solution.py:36
  24.8 3.0 fusion.30
  27.8 1.6 copy.14
  29.4 63.3 %reduce-scatter.2.cloned.1.call-done = f32[4,64,128]{2,1,0:T(8,128)} async-done(((f32[32,64,128]{2,1,0:T(8,128)}), f32[4,64,128]{2,1,0:T(8,128)}) %reduce-scatter.2.cloned.1.call-update) | async-done | bytes 131088 | tf_op jit(solution)/shard_map/while/body/eval_jaxpr/reduce_scatter | solution.py:39
  92.6 1.3 collective-permute-start
  94.0 3.8 %collective-permute-done = f32[4,64,128]{2,1,0:T(8,128)S(1)} collective-permute-done((f32[4,64,128]{2,1,0:T(8,128)}, f32[4,64,128]{2,1,0:T(8,128)S(1)}, u32[]{:S(2)}, u32[]{:S(2)}) %collective-permute-start) | collective-permute-done | bytes 131104 | tf_op jit(solution)/shard_map/while/body/eval_jaxpr/ppermute | solution.py:10
  97.8 1.6 select_select_fusion.4
  100.1 0.7 gather_fusion
  100.9 13.7 %fusion.29 = f32[94,64,128]{2,1,0:T(8,128)S(1)} fusion(f32[94,128,128]{2,1,0:T(8,128)} %get-tuple-element.327, f32[94,64,128]{2,1,0:T(8,128)S(1)} %gather_fusion, pred[94]{0:T(512)(128)(4,1)S(1)} %compare_and_fusion.2), kind=kOutput, calls=%fused_computation.3.clone.1 | convolution fusion | flops 1183563776 | bytes 12320862 | tf_op jit(solution)/shard_map/while/body/eval_jaxpr/krc,ksc->ksr/dot_general | solution.py:36
  114.6 3.0 fusion.30
  117.6 1.6 copy.14
  119.2 64.0 %reduce-scatter.2.cloned.1.call-done = f32[4,64,128]{2,1,0:T(8,128)} async-done(((f32[32,64,128]{2,1,0:T(8,128)}), f32[4,64,128]{2,1,0:T(8,128)}) %reduce-scatter.2.cloned.1.call-update) | async-done | bytes 131088 | tf_op jit(solution)/shard_map/while/body/eval_jaxpr/reduce_scatter | solution.py:39
  183.2 1.3 collective-permute-start
  184.6 3.8 %collective-permute-done = f32[4,64,128]{2,1,0:T(8,128)S(1)} collective-permute-done((f32[4,64,128]{2,1,0:T(8,128)}, f32[4,64,128]{2,1,0:T(8,128)S(1)}, u32[]{:S(2)}, u32[]{:S(2)}) %collective-permute-start) | collective-permute-done | bytes 131104 | tf_op jit(solution)/shard_map/while/body/eval_jaxpr/ppermute | solution.py:10
  188.4 1.6 select_select_fusion.4
  191.5 13.7 %fusion.29 = f32[94,64,128]{2,1,0:T(8,128)S(1)} fusion(f32[94,128,128]{2,1,0:T(8,128)} %get-tuple-element.327, f32[94,64,128]{2,1,0:T(8,128)S(1)} %gather_fusion, pred[94]{0:T(512)(128)(4,1)S(1)} %compare_and_fusion.2), kind=kOutput, calls=%fused_computation.3.clone.1 | convolution fusion | flops 1183563776 | bytes 12320862 | tf_op jit(solution)/shard_map/while/body/eval_jaxpr/krc,ksc->ksr/dot_general | solution.py:36
  205.2 3.0 fusion.30
  208.2 1.6 copy.14
  209.8 64.0 %reduce-scatter.2.cloned.1.call-done = f32[4,64,128]{2,1,0:T(8,128)} async-done(((f32[32,64,128]{2,1,0:T(8,128)}), f32[4,64,128]{2,1,0:T(8,128)}) %reduce-scatter.2.cloned.1.call-update) | async-done | bytes 131088 | tf_op jit(solution)/shard_map/while/body/eval_jaxpr/reduce_scatter | solution.py:39
  273.8 1.3 collective-permute-start
  275.1 3.8 %collective-permute-done = f32[4,64,128]{2,1,0:T(8,128)S(1)} collective-permute-done((f32[4,64,128]{2,1,0:T(8,128)}, f32[4,64,128]{2,1,0:T(8,128)S(1)}, u32[]{:S(2)}, u32[]{:S(2)}) %collective-permute-start) | collective-permute-done | bytes 131104 | tf_op jit(solution)/shard_map/while/body/eval_jaxpr/ppermute | solution.py:10
  279.0 1.6 select_select_fusion.4
  282.1 13.7 %fusion.29 = f32[94,64,128]{2,1,0:T(8,128)S(1)} fusion(f32[94,128,128]{2,1,0:T(8,128)} %get-tuple-element.327, f32[94,64,128]{2,1,0:T(8,128)S(1)} %gather_fusion, pred[94]{0:T(512)(128)(4,1)S(1)} %compare_and_fusion.2), kind=kOutput, calls=%fused_computation.3.clone.1 | convolution fusion | flops 1183563776 | bytes 12320862 | tf_op jit(solution)/shard_map/while/body/eval_jaxpr/krc,ksc->ksr/dot_general | solution.py:36
  295.8 3.0 fusion.30
  298.8 1.6 copy.14
  300.4 64.0 %reduce-scatter.2.cloned.1.call-done = f32[4,64,128]{2,1,0:T(8,128)} async-done(((f32[32,64,128]{2,1,0:T(8,128)}), f32[4,64,128]{2,1,0:T(8,128)}) %reduce-scatter.2.cloned.1.call-update) | async-done | bytes 131088 | tf_op jit(solution)/shard_map/while/body/eval_jaxpr/reduce_scatter | solution.py:39
  364.4 1.3 collective-permute-start
  365.7 1.0 select_select_fusion.5
  366.6 2.9 collective-permute-done
  (57 shorter events, 5.8 us)
Async XLA Ops:
  7.9 84.8 %reduce-scatter.2.cloned.1.call-start = ((), (), s32[]{:S(2)}) async-start(), calls=%async_computation.1 | async-start | bytes 1179648 | tf_op jit(solution)/shard_map/while/body/eval_jaxpr/reduce_scatter | solution.py:39
  9.6 0.7 copy-start.1
  11.0 13.7 %copy-start.4 = (s32[1,94]{1,0:T(1,128)S(1)}, s32[1,94]{1,0:T(1,128)}, u32[]{:S(2)}) copy-start(s32[1,94]{1,0:T(1,128)} %get-tuple-element.325) | copy-start | bytes 1132 | tf_op jit(solution)/shard_map/while
  24.7 73.0 %copy-start.2 = (f32[4,64,128]{2,1,0:T(8,128)S(1)}, f32[4,64,128]{2,1,0:T(8,128)}, u32[]{:S(2)}) copy-start(f32[4,64,128]{2,1,0:T(8,128)} %copy-done.1) | copy-start | bytes 393220 | tf_op jit(solution)/shard_map/while
  92.6 5.1 %collective-permute-start = (f32[4,64,128]{2,1,0:T(8,128)}, f32[4,64,128]{2,1,0:T(8,128)S(1)}, u32[]{:S(2)}, u32[]{:S(2)}) collective-permute-start(f32[4,64,128]{2,1,0:T(8,128)} %reduce-scatter.2.cloned.1.call-done), channel_id=1, source_target_pairs={{0,8},{8,16},{16,24},{1,9},{9,17},{17,25},{2,10},{10,18},{18,26},{... | collective-permute-start | bytes 393224 | tf_op jit(solution)/shard_map/while/body/eval_jaxpr/ppermute | solution.py:10
  97.8 85.4 %reduce-scatter.2.cloned.1.call-start = ((), (), s32[]{:S(2)}) async-start(), calls=%async_computation.1 | async-start | bytes 1179648 | tf_op jit(solution)/shard_map/while/body/eval_jaxpr/reduce_scatter | solution.py:39
  99.5 0.7 copy-start.1
  100.9 13.7 %copy-start.4 = (s32[1,94]{1,0:T(1,128)S(1)}, s32[1,94]{1,0:T(1,128)}, u32[]{:S(2)}) copy-start(s32[1,94]{1,0:T(1,128)} %get-tuple-element.325) | copy-start | bytes 1132 | tf_op jit(solution)/shard_map/while
  114.6 73.8 %copy-start.2 = (f32[4,64,128]{2,1,0:T(8,128)S(1)}, f32[4,64,128]{2,1,0:T(8,128)}, u32[]{:S(2)}) copy-start(f32[4,64,128]{2,1,0:T(8,128)} %copy-done.1) | copy-start | bytes 393220 | tf_op jit(solution)/shard_map/while
  183.2 5.2 %collective-permute-start = (f32[4,64,128]{2,1,0:T(8,128)}, f32[4,64,128]{2,1,0:T(8,128)S(1)}, u32[]{:S(2)}, u32[]{:S(2)}) collective-permute-start(f32[4,64,128]{2,1,0:T(8,128)} %reduce-scatter.2.cloned.1.call-done), channel_id=1, source_target_pairs={{0,8},{8,16},{16,24},{1,9},{9,17},{17,25},{2,10},{10,18},{18,26},{... | collective-permute-start | bytes 393224 | tf_op jit(solution)/shard_map/while/body/eval_jaxpr/ppermute | solution.py:10
  188.4 85.4 %reduce-scatter.2.cloned.1.call-start = ((), (), s32[]{:S(2)}) async-start(), calls=%async_computation.1 | async-start | bytes 1179648 | tf_op jit(solution)/shard_map/while/body/eval_jaxpr/reduce_scatter | solution.py:39
  190.1 0.7 copy-start.1
  191.5 13.7 %copy-start.4 = (s32[1,94]{1,0:T(1,128)S(1)}, s32[1,94]{1,0:T(1,128)}, u32[]{:S(2)}) copy-start(s32[1,94]{1,0:T(1,128)} %get-tuple-element.325) | copy-start | bytes 1132 | tf_op jit(solution)/shard_map/while
  205.2 73.7 %copy-start.2 = (f32[4,64,128]{2,1,0:T(8,128)S(1)}, f32[4,64,128]{2,1,0:T(8,128)}, u32[]{:S(2)}) copy-start(f32[4,64,128]{2,1,0:T(8,128)} %copy-done.1) | copy-start | bytes 393220 | tf_op jit(solution)/shard_map/while
  273.8 5.1 %collective-permute-start = (f32[4,64,128]{2,1,0:T(8,128)}, f32[4,64,128]{2,1,0:T(8,128)S(1)}, u32[]{:S(2)}, u32[]{:S(2)}) collective-permute-start(f32[4,64,128]{2,1,0:T(8,128)} %reduce-scatter.2.cloned.1.call-done), channel_id=1, source_target_pairs={{0,8},{8,16},{16,24},{1,9},{9,17},{17,25},{2,10},{10,18},{18,26},{... | collective-permute-start | bytes 393224 | tf_op jit(solution)/shard_map/while/body/eval_jaxpr/ppermute | solution.py:10
  278.9 85.5 %reduce-scatter.2.cloned.1.call-start = ((), (), s32[]{:S(2)}) async-start(), calls=%async_computation.1 | async-start | bytes 1179648 | tf_op jit(solution)/shard_map/while/body/eval_jaxpr/reduce_scatter | solution.py:39
  280.6 0.7 copy-start.1
  282.1 13.7 %copy-start.4 = (s32[1,94]{1,0:T(1,128)S(1)}, s32[1,94]{1,0:T(1,128)}, u32[]{:S(2)}) copy-start(s32[1,94]{1,0:T(1,128)} %get-tuple-element.325) | copy-start | bytes 1132 | tf_op jit(solution)/shard_map/while
  295.8 73.8 %copy-start.2 = (f32[4,64,128]{2,1,0:T(8,128)S(1)}, f32[4,64,128]{2,1,0:T(8,128)}, u32[]{:S(2)}) copy-start(f32[4,64,128]{2,1,0:T(8,128)} %copy-done.1) | copy-start | bytes 393220 | tf_op jit(solution)/shard_map/while
  364.4 5.1 %collective-permute-start = (f32[4,64,128]{2,1,0:T(8,128)}, f32[4,64,128]{2,1,0:T(8,128)S(1)}, u32[]{:S(2)}, u32[]{:S(2)}) collective-permute-start(f32[4,64,128]{2,1,0:T(8,128)} %reduce-scatter.2.cloned.1.call-done), channel_id=1, source_target_pairs={{0,8},{8,16},{16,24},{1,9},{9,17},{17,25},{2,10},{10,18},{18,26},{... | collective-permute-start | bytes 393224 | tf_op jit(solution)/shard_map/while/body/eval_jaxpr/ppermute | solution.py:10
  369.5 0.7 copy-start
  369.5 0.7 copy-start.3
Sparse Core Ops, SparseCore 0:
  29.5 63.1 reduce-scatter.1
  119.3 63.8 reduce-scatter.1
  209.9 63.7 reduce-scatter.1
  300.5 63.8 reduce-scatter.1
where the time goes:
time: 380 us; the launch traced here: 377 us
  waiting for transfers between devices  270 us (71%)
  matrix products  73.3 us (19%)
  between operations  13.7 us (4%)
  local copies, waits for them, and re-layouts  12.7 us (3%)
  starting transfers between devices  5.17 us (1%)
    reduce_scatter x4, waiting for transfers between devices, advance(): lax.psum_scatter(jnp.einsum('kt,ksr->tsr', onehot, products, precision=hi...  255 us
    dot_general x4, matrix products, advance(): products = jnp.einsum('krc,ksc->ksr', factor, picked, precision=highest)  54.7 us
    ppermute x4, waiting for transfers between devices, shifted(): return lax.ppermute(block, axis, route)  14.3 us
    dot_general x4, matrix products, advance(): jnp.einsum('kt,ksr->tsr', onehot, products, precision=highest)  12 us
  transfers between devices with their start and end apart: 8, of which 8 were waited for; matrix products, arithmetic and copies ran while one was open for 0% of the time, Pallas kernels for 0%

commit v1 on v0

v1 whole, which is shorter than its diff:
```python
import functools

import jax
import jax.numpy as jnp
from jax import lax
from jax.experimental import pallas as pl
from jax.experimental.pallas import tpu as pltpu
from jax.sharding import PartitionSpec as P

MESH = pl.DeviceIdType.MESH
MIB = 1 << 20


def split(value):
    high = value.astype(jnp.bfloat16)
    low = (value - high.astype(jnp.float32)).astype(jnp.bfloat16)
    return high, low


def times_transposed(left, right):
    return lax.dot_general(left, right, (((1,), (1,)), ((), ())), preferred_element_type=jnp.float32)


def merge_kernel(chunk, tiles, rows_ref, cols_ref, factor_ref, high_ref, low_ref, total):
    step = pl.program_id(0)
    size = factor_ref.shape[-1]
    width = high_ref.shape[-1] // size
    blocks = high_ref.shape[0] // size

    @pl.when(step == 0)
    def _():
        def clear(block, carry):
            at = pl.ds(pl.multiple_of(block * size, size), size)
            total[at, :] = jnp.zeros((size, total.shape[1]), jnp.float32)
            return carry

        lax.fori_loop(0, blocks, clear, 0)

    def add(j, carry):
        k = step * chunk + j
        row = pl.ds(pl.multiple_of(rows_ref[k] * size, size), size)
        col = pl.ds(pl.multiple_of(cols_ref[k] * size, size), size)
        total[row, col] += factor_ref[j]
        return carry

    lax.fori_loop(0, jnp.minimum(chunk, tiles - step * chunk), add, 0)

    @pl.when(step == pl.num_programs(0) - 1)
    def _():
        def finish(block, carry):
            at = pl.ds(pl.multiple_of(block * size, size), size)
            for c in range(width):
                cs = slice(c * size, (c + 1) * size)
                high, low = split(total[at, cs])
                high_ref[at, cs] = high
                low_ref[at, cs] = low
            return carry

        lax.fori_loop(0, blocks, finish, 0)


def merge(factor, rows, cols, row_tiles, col_tiles):
    tiles, size, _ = factor.shape
    chunk = 16
    shape = (row_tiles * size, col_tiles * size)
    whole = pl.BlockSpec(memory_space=pltpu.VMEM)
    return pl.pallas_call(
        functools.partial(merge_kernel, chunk, tiles),
        out_shape=[pltpu.VMEM(shape, jnp.bfloat16)] * 2,
        grid_spec=pltpu.PrefetchScalarGridSpec(
            num_scalar_prefetch=2,
            grid=(pl.cdiv(tiles, chunk),),
            in_specs=[pl.BlockSpec((chunk, size, size), lambda i, *_: (i, 0, 0))],
            out_specs=[whole] * 2,
            scratch_shapes=[pltpu.VMEM(shape, jnp.float32)],
        ),
        compiler_params=pltpu.CompilerParams(
            dimension_semantics=("arbitrary",), vmem_limit_bytes=24 * MIB + 2 * shape[0] * shape[1]
        ),
    )(rows, cols, factor)


def chain_kernel(
    groups, nx, nz,
    src_ref, inv_ref, high_ref, low_ref, solved_ref, leaving_ref,
    panel, own, xout, xin, zout, zin, zlast, bout, bin_,
    xsend, xrecv, zsend, zrecv, lrecv, bsend, brecv,
):
    g = lax.axis_index("chain")
    col = lax.axis_index("col")
    x = lax.rem(col, nx)
    z = lax.div(col, nx)
    per, sources, size = src_ref.shape
    last = g == groups - 1

    def place(dx, dz):
        return lax.rem(z + dz, nz) * nx + lax.rem(x + dx, nx)

    barrier = pltpu.get_barrier_semaphore()

    def greet(chain, dx, dz):
        pl.semaphore_signal(barrier, inc=1, device_id=(chain, place(dx, dz)), device_id_type=MESH)

    for dx in range(1, nx):
        greet(g, dx, 0)

    @pl.when(g > 0)
    def _():
        for dz in range(nz):
            greet(g - 1, 0, dz)

    @pl.when(jnp.logical_not(last))
    def _():
        for dz in range(nz):
            greet(g + 1, 0, dz)

    @pl.when(last)
    def _():
        for dz in range(1, nz):
            greet(g, 0, dz)

    awaited = (nx - 1) + jnp.where(g > 0, nz, 0) + jnp.where(last, nz - 1, nz)
    pl.semaphore_wait(barrier, awaited)

    def x_copy(dx, dz):
        return pltpu.make_async_remote_copy(
            src_ref=xout.at[dx - 1, dz], dst_ref=xin.at[dx - 1, dz],
            send_sem=xsend.at[dx - 1, dz], recv_sem=xrecv.at[dx - 1, dz],
            device_id=(g, place(dx, 0)), device_id_type=MESH,
        )

    def z_copy(dz):
        return pltpu.make_async_remote_copy(
            src_ref=zout.at[dz], dst_ref=zin.at[dz],
            send_sem=zsend.at[dz], recv_sem=zrecv.at[dz],
            device_id=(g + 1, place(0, dz)), device_id_type=MESH,
        )

    def last_copy(dz):
        return pltpu.make_async_remote_copy(
            src_ref=zout.at[dz], dst_ref=zlast.at[dz],
            send_sem=zsend.at[dz], recv_sem=lrecv.at[dz],
            device_id=(g, place(0, dz)), device_id_type=MESH,
        )

    back = pltpu.make_async_remote_copy(
        src_ref=bout, dst_ref=bin_, send_sem=bsend, recv_sem=brecv,
        device_id=(g - 1, col), device_id_type=MESH,
    )

    @pl.when(g == 0)
    def _():
        bout[...] = jnp.zeros(bout.shape, jnp.float32)

    @pl.when(g > 0)
    def _():
        for dz in range(nz):
            z_copy(dz).wait_recv()
        total = zin[0]
        for dz in range(1, nz):
            total = total + zin[dz]
        bout[...] = total
        back.start()

    for t in range(per):
        right, rest = split(src_ref[t] - bout[t])
        inv, inv_rest = split(inv_ref[t])
        both = times_transposed(jnp.concatenate([right, rest], axis=0), inv)
        current = both[:sources] + both[sources:] + times_transposed(right, inv_rest)
        solved_ref[t] = current
        high, low = split(current)
        panel[:sources, t * size:(t + 1) * size] = high
        panel[sources:, t * size:(t + 1) * size] = low

    def chunk(dx, dz, store):
        rows = per * size
        at = pl.ds(pl.multiple_of(place(dx, dz) * rows, rows), rows)
        both = times_transposed(panel[...], high_ref[at, :])
        result = both[:sources] + both[sources:] + times_transposed(panel[:sources, :], low_ref[at, :])
        for t in range(per):
            store[t] = result[:, t * size:(t + 1) * size]

    order = sorted(range(1, nz), key=lambda d: abs(2 * d - nz)) + [0]
    for dz in order:
        for dx in range(1, nx):
            chunk(dx, dz, xout.at[dx - 1, dz])
            x_copy(dx, dz).start()
    for dz in order:
        chunk(0, dz, own.at[dz])
    for dz in order:
        for dx in range(1, nx):
            x_copy(dx, dz).wait_recv()
        for t in range(per):
            part = own[dz, t]
            for dx in range(1, nx):
                part = part + xin[dx - 1, dz, t]
            zout[dz, t] = part

        @pl.when(jnp.logical_not(last))
        def _():
            z_copy(dz).start()

        if dz > 0:
            @pl.when(last)
            def _():
                last_copy(dz).start()

    @pl.when(last)
    def _():
        for dz in range(1, nz):
            last_copy(dz).wait_recv()
        total = zout[0]
        for dz in range(1, nz):
            total = total + zlast[dz]
        leaving_ref[...] = total
        for dz in range(1, nz):
            last_copy(dz).wait_send()

    @pl.when(jnp.logical_not(last))
    def _():
        back.wait_recv()
        leaving_ref[...] = bin_[...]
        for dz in range(nz):
            z_copy(dz).wait_send()

    for dz in order:
        for dx in range(1, nx):
            x_copy(dx, dz).wait_send()

    @pl.when(g > 0)
    def _():
        back.wait_send()


def local(nx, groups, col_devices, sources, diag_inverse, factor_tiles, tile_rows, tile_cols):
    per, panel_sources, size = sources.shape[1:]
    nz = col_devices // nx
    local_cols = tile_cols[0] - lax.axis_index("col") * per
    high, low = merge(factor_tiles[0], tile_rows[0], local_cols, per * col_devices, per)
    block = (per, panel_sources, size)
    whole = pl.BlockSpec(memory_space=pltpu.VMEM)
    dma = pltpu.SemaphoreType.DMA
    solved, leaving = pl.pallas_call(
        functools.partial(chain_kernel, groups, nx, nz),
        out_shape=[jax.ShapeDtypeStruct(block, jnp.float32)] * 2,
        in_specs=[whole] * 4,
        out_specs=[whole] * 2,
        scratch_shapes=[
            pltpu.VMEM((2 * panel_sources, per * size), jnp.bfloat16),
            pltpu.VMEM((nz,) + block, jnp.float32),
            pltpu.VMEM((nx - 1, nz) + block, jnp.float32),
            pltpu.VMEM((nx - 1, nz) + block, jnp.float32),
            pltpu.VMEM((nz,) + block, jnp.float32),
            pltpu.VMEM((nz,) + block, jnp.float32),
            pltpu.VMEM((nz,) + block, jnp.float32),
            pltpu.VMEM(block, jnp.float32),
            pltpu.VMEM(block, jnp.float32),
            dma((nx - 1, nz)),
            dma((nx - 1, nz)),
            dma((nz,)),
            dma((nz,)),
            dma((nz,)),
            dma(()),
            dma(()),
        ],
        compiler_params=pltpu.CompilerParams(
            collective_id=0, has_side_effects=True, vmem_limit_bytes=36 * MIB
        ),
    )(sources[0], diag_inverse[0], high, low)
    return (solved[None], leaving[None])


def solution(mesh):
    groups, col_devices = mesh.shape["chain"], mesh.shape["col"]
    nx = max(d for d in range(1, col_devices + 1) if col_devices % d == 0 and d * d <= col_devices)
    return jax.shard_map(
        functools.partial(local, nx, groups, col_devices),
        mesh=mesh,
        in_specs=(
            P("chain", "col", None, None),
            P("chain", "col", None, None),
            P("chain", "col", None, None),
            P("chain", "col"),
            P("chain", "col"),
        ),
        out_specs=(P("chain", "col", None, None), P("chain", "col", None, None)),
        check_vma=False,
    )
```

time: 380 us -> 62.3 us (0.16)
  waiting for transfers between devices: 270 us -> 0 us
  matrix products: 73.3 us -> 0 us
  Pallas kernels: 0 us -> 56 us
  between operations: 13.7 us -> 0.67 us
  local copies, waits for them, and re-layouts: 12.7 us -> 4.72 us
  starting transfers between devices: 5.17 us -> 0 us
    reduce_scatter x4 -> x0, waiting for transfers between devices: 255 us -> none  [advance(): lax.psum_scatter(jnp.einsum('kt,ksr->tsr', onehot, products, precision=hi...]
    dot_general x12 -> x0, matrix products: 73.3 us -> none  [the longest x4 54.7 us: advance(): products = jnp.einsum('krc,ksc->ksr', factor, picked, precision=highest)]
    pallas_call x0 -> x2, Pallas kernels: none -> 56 us  [the longest x1 51.6 us: local(): pl.pallas_call(functools.partial(chain_kernel, groups, nx, nz), out_shape...]
    ppermute x4 -> x0, waiting for transfers between devices: 14.3 us -> none  [shifted(): return lax.ppermute(block, axis, route)]
    dot_general x4 -> x0, local copies, waits for them, and re-layouts: 6.31 us -> none  [advance(): jnp.einsum('kt,ksr->tsr', onehot, products, precision=highest)]
    ppermute x4 -> x0, starting transfers between devices: 5.12 us -> none  [shifted(): return lax.ppermute(block, axis, route)]
    unnamed x4 -> x10, local copies, waits for them, and re-layouts: 0.7 us -> 4.72 us
  transfers between devices with their start and end apart: 8 -> 0, of which waited for: 8 -> 0; matrix products, arithmetic and copies ran while one was open for 0% -> 0% of each run, Pallas kernels for 0% -> 0%
where the time goes in v1:
time: 62.3 us; the launch traced here: 62.1 us
  Pallas kernels  56 us (90%)
  local copies, waits for them, and re-layouts  4.72 us (8%)
  between operations  0.67 us (1%)
  other arithmetic  0.66 us (1%)
    pallas_call x1, Pallas kernels, local(): pl.pallas_call(functools.partial(chain_kernel, groups, nx, nz), out_shape...  51.6 us
    unnamed x10, local copies, waits for them, and re-layouts  4.72 us
    pallas_call x1, Pallas kernels, merge(): pl.pallas_call(functools.partial(merge_kernel, chunk, tiles), out_shape=[...  4.41 us

profile of v1, /device:TPU:5, one launch (start us, length us, event | category | flops | bytes accessed | tf_op | source)
XLA Modules:
  0.0 62.1 jit_solution(10958361741386540111)
XLA Ops:
  0.6 0.7 %subtract_bitcast_fusion.cols_ref = s32[94]{0:T(128)S(1)} fusion(s32[1,94]{1,0:T(1,128)} %param.9, s32[]{:T(128)S(6)} %mul.3), kind=kLoop, calls=%fused_computation | loop fusion | flops 94 | bytes 756 | tf_op jit(solution)/shard_map/sub | solution.py:238
  1.3 0.0 copy-start
  1.3 2.7 %copy-done = f32[1,94,128,128]{3,2,1,0:T(8,128)S(1)} copy-done((f32[1,94,128,128]{3,2,1,0:T(8,128)S(1)}, f32[1,94,128,128]{3,2,1,0:T(8,128)}, u32[]{:S(2)}) %copy-start) | copy-done | bytes 6160408
  4.0 0.0 copy-start.3
  4.0 0.7 %copy-done.3 = s32[1,94]{1,0:T(1,128)S(1)} copy-done((s32[1,94]{1,0:T(1,128)S(1)}, s32[1,94]{1,0:T(1,128)}, u32[]{:S(2)}) %copy-start.3) | copy-done | bytes 400
  4.7 0.0 copy-start.1
  4.7 0.0 copy-start.2
  4.7 4.4 %shard_map.68 = (bf16[4096,512]{1,0:T(8,128)(2,1)S(1)}, bf16[4096,512]{1,0:T(8,128)(2,1)S(1)}) custom-call(s32[94]{0:T(128)S(1)} %bitcast.13, s32[94]{0:T(128)S(1)} %subtract_bitcast_fusion.cols_ref, f32[94,128,128]{2,1,0:T(8,128)S(1)} %bitcast.8), custom_call_target="tpu_custom_call" | custom-call | tf_op jit(solution)/shard_map/pallas_call | solution.py:67
  9.1 0.0 copy-done.1
  9.1 0.0 copy-done.2
  9.1 51.6 %shard_map.69 = (f32[4,64,128]{2,1,0:T(8,128)S(1)}, f32[4,64,128]{2,1,0:T(8,128)S(1)}) custom-call(f32[4,64,128]{2,1,0:T(8,128)S(1)} %bitcast.10, f32[4,128,128]{2,1,0:T(8,128)S(1)} %bitcast.9, bf16[4096,512]{1,0:T(8,128)(2,1)S(1)} %get-tuple-element.6.high_ref, bf16[4096,512]{1,0:T(8,128)(2,1)S(1)} %get-tuple-element.7.low_ref), custom_call_target="tpu_custom_call" | custom-call | tf_op jit(solution)/shard_map/pallas_call | solution.py:243
  60.8 0.7 %copy.9 = f32[1,4,64,128]{3,2,1,0:T(8,128)} copy(f32[1,4,64,128]{3,2,1,0:T(8,128)S(1)} %bitcast.12) | data formatting | bytes 262144
  61.4 0.7 %copy.10 = f32[1,4,64,128]{3,2,1,0:T(8,128)} copy(f32[1,4,64,128]{3,2,1,0:T(8,128)S(1)} %bitcast.11) | data formatting | bytes 262144
Async XLA Ops:
  1.3 2.7 %copy-start = (f32[1,94,128,128]{3,2,1,0:T(8,128)S(1)}, f32[1,94,128,128]{3,2,1,0:T(8,128)}, u32[]{:S(2)}) copy-start(f32[1,94,128,128]{3,2,1,0:T(8,128)} %param.7) | copy-start | bytes 18481156
  4.0 0.7 %copy-start.3 = (s32[1,94]{1,0:T(1,128)S(1)}, s32[1,94]{1,0:T(1,128)}, u32[]{:S(2)}) copy-start(s32[1,94]{1,0:T(1,128)} %param.8) | copy-start | bytes 1132
  4.7 4.4 %copy-start.1 = (f32[1,4,128,128]{3,2,1,0:T(8,128)S(1)}, f32[1,4,128,128]{3,2,1,0:T(8,128)}, u32[]{:S(2)}) copy-start(f32[1,4,128,128]{3,2,1,0:T(8,128)} %param.6) | copy-start | bytes 786436
  4.7 4.4 %copy-start.2 = (f32[1,4,64,128]{3,2,1,0:T(8,128)S(1)}, f32[1,4,64,128]{3,2,1,0:T(8,128)}, u32[]{:S(2)}) copy-start(f32[1,4,64,128]{3,2,1,0:T(8,128)} %param.5) | copy-start | bytes 393220

commit v2 on v0

v2 whole, which is shorter than its diff:
```python
import functools

import jax
import jax.numpy as jnp
from jax import lax
from jax.experimental import pallas as pl
from jax.experimental.pallas import tpu as pltpu
from jax.sharding import PartitionSpec as P

MESH = pl.DeviceIdType.MESH
MIB = 1 << 20
PANELS = 4


def split(value):
    high = value.astype(jnp.bfloat16)
    low = (value - high.astype(jnp.float32)).astype(jnp.bfloat16)
    return high, low


def times_transposed(left, right):
    return lax.dot_general(left, right, (((1,), (1,)), ((), ())), preferred_element_type=jnp.float32)


def merge_kernel(pieces, rows_ref, cols_ref, factor_ref, high_ref, low_ref, held, total, arrived):
    tiles, size, _ = factor_ref.shape
    width = high_ref.shape[1] // size
    blocks = high_ref.shape[0] // size

    def fetch(i):
        span = pl.ds(pieces[i], pieces[i + 1] - pieces[i])
        return pltpu.make_async_copy(factor_ref.at[span], held.at[span], arrived.at[i])

    for i in range(len(pieces) - 1):
        fetch(i).start()

    def clear(block, carry):
        at = pl.ds(pl.multiple_of(block * size, size), size)
        total[at, :] = jnp.zeros((size, total.shape[1]), jnp.float32)
        return carry

    lax.fori_loop(0, blocks, clear, 0)

    def add(k, carry):
        row = pl.ds(pl.multiple_of(rows_ref[0, k] * size, size), size)
        col = pl.ds(pl.multiple_of(lax.rem(cols_ref[0, k], width) * size, size), size)
        total[row, col] += held[k]
        return carry

    for i in range(len(pieces) - 1):
        fetch(i).wait()
        lax.fori_loop(pieces[i], pieces[i + 1], add, 0)

    def finish(block, carry):
        at = pl.ds(pl.multiple_of(block * size, size), size)
        for c in range(width):
            cs = slice(c * size, (c + 1) * size)
            high, low = split(total[at, cs])
            high_ref[at, cs] = high
            low_ref[at, cs] = low
        return carry

    lax.fori_loop(0, blocks, finish, 0)


def merge(factor, rows, cols, row_tiles, col_tiles):
    tiles, size, _ = factor.shape
    pieces = list(range(0, tiles, 16)) + [tiles]
    shape = (row_tiles * size, col_tiles * size)
    whole = pl.BlockSpec(memory_space=pltpu.VMEM)
    scalars = pl.BlockSpec(memory_space=pltpu.SMEM)
    return pl.pallas_call(
        functools.partial(merge_kernel, pieces),
        out_shape=[pltpu.VMEM(shape, jnp.bfloat16)] * 2,
        in_specs=[scalars, scalars, pl.BlockSpec(memory_space=pltpu.HBM)],
        out_specs=[whole] * 2,
        scratch_shapes=[
            pltpu.VMEM(factor.shape, jnp.float32),
            pltpu.VMEM(shape, jnp.float32),
            pltpu.SemaphoreType.DMA((len(pieces) - 1,)),
        ],
        compiler_params=pltpu.CompilerParams(vmem_limit_bytes=40 * MIB),
    )(*(pltpu.with_memory_space_constraint(a, pltpu.HBM) for a in (rows, cols, factor)))


def chain_kernel(
    groups, nx, nz, panels,
    src_ref, inv_ref, high_ref, low_ref, solved_ref, leaving_ref,
    inv_high, inv_low, operand, own, xout, xin, zout, zin, zlast, bout, bin_,
    xsend, xrecv, zsend, zrecv, lrecv, bsend, brecv,
):
    g = lax.axis_index("chain")
    col = lax.axis_index("col")
    x = lax.rem(col, nx)
    z = lax.div(col, nx)
    per, sources, size = src_ref.shape
    wide = sources // panels
    last = g == groups - 1
    inner = jnp.logical_not(last)

    def place(dx, dz):
        return lax.rem(z + dz, nz) * nx + lax.rem(x + dx, nx)

    barrier = pltpu.get_barrier_semaphore()

    def greet(chain, dx, dz):
        pl.semaphore_signal(barrier, inc=1, device_id=(chain, place(dx, dz)), device_id_type=MESH)

    for dx in range(1, nx):
        greet(g, dx, 0)

    @pl.when(g > 0)
    def _():
        for dz in range(nz):
            greet(g - 1, 0, dz)

    @pl.when(inner)
    def _():
        for dz in range(nz):
            greet(g + 1, 0, dz)

    @pl.when(last)
    def _():
        for dz in range(1, nz):
            greet(g, 0, dz)

    for t in range(per):
        inv_high[t], inv_low[t] = split(inv_ref[t])

    @pl.when(g == 0)
    def _():
        bout[...] = jnp.zeros(bout.shape, jnp.float32)

    awaited = (nx - 1) + jnp.where(g > 0, nz, 0) + jnp.where(last, nz - 1, nz)
    pl.semaphore_wait(barrier, awaited)

    def x_copy(p, dx, dz):
        return pltpu.make_async_remote_copy(
            src_ref=xout.at[p, dx - 1, dz], dst_ref=xin.at[p, dx - 1, dz],
            send_sem=xsend.at[p, dx - 1, dz], recv_sem=xrecv.at[p, dx - 1, dz],
            device_id=(g, place(dx, 0)), device_id_type=MESH,
        )

    def z_copy(p, dz):
        return pltpu.make_async_remote_copy(
            src_ref=zout.at[p, dz], dst_ref=zin.at[p, dz],
            send_sem=zsend.at[p, dz], recv_sem=zrecv.at[p, dz],
            device_id=(g + 1, place(0, dz)), device_id_type=MESH,
        )

    def last_copy(p, dz):
        return pltpu.make_async_remote_copy(
            src_ref=zout.at[p, dz], dst_ref=zlast.at[p, dz],
            send_sem=zsend.at[p, dz], recv_sem=lrecv.at[p, dz],
            device_id=(g, place(0, dz)), device_id_type=MESH,
        )

    def back(p):
        return pltpu.make_async_remote_copy(
            src_ref=bout.at[p], dst_ref=bin_.at[p],
            send_sem=bsend.at[p], recv_sem=brecv.at[p],
            device_id=(g - 1, col), device_id_type=MESH,
        )

    order = sorted(range(1, nz), key=lambda d: abs(2 * d - nz)) + [0]

    def chunk(dx, dz):
        rows = per * size
        at = pl.ds(pl.multiple_of(place(dx, dz) * rows, rows), rows)
        both = times_transposed(operand[...], high_ref[at, :])
        return both[:wide] + both[wide:] + times_transposed(operand[:wide, :], low_ref[at, :])

    def first(p):
        @pl.when(g > 0)
        def _():
            for dz in range(nz):
                z_copy(p, dz).wait_recv()
            total = zin[p, 0]
            for dz in range(1, nz):
                total = total + zin[p, dz]
            bout[p] = total
            back(p).start()

        span = pl.ds(pl.multiple_of(p * wide, wide), wide)
        for t in range(per):
            right, rest = split(src_ref[t, span, :] - bout[p, t])
            both = times_transposed(jnp.concatenate([right, rest], axis=0), inv_high[t])
            current = both[:wide] + both[wide:] + times_transposed(right, inv_low[t])
            solved_ref[t, span, :] = current
            high, low = split(current)
            operand[:wide, t * size:(t + 1) * size] = high
            operand[wide:, t * size:(t + 1) * size] = low

        for dz in order:
            for dx in range(1, nx):
                result = chunk(dx, dz)
                for t in range(per):
                    xout[p, dx - 1, dz, t] = result[:, t * size:(t + 1) * size]
                x_copy(p, dx, dz).start()
        for dz in order:
            result = chunk(0, dz)
            for t in range(per):
                own[p, dz, t] = result[:, t * size:(t + 1) * size]

    def second(p):
        for dz in order:
            for dx in range(1, nx):
                x_copy(p, dx, dz).wait_recv()
            part = own[p, dz]
            for dx in range(1, nx):
                part = part + xin[p, dx - 1, dz]
            zout[p, dz] = part

            @pl.when(inner)
            def _():
                z_copy(p, dz).start()

            if dz > 0:
                @pl.when(last)
                def _():
                    last_copy(p, dz).start()

    def tick(moment, carry):
        @pl.when(moment < panels)
        def _():
            first(moment)

        @pl.when(moment > 0)
        def _():
            second(moment - 1)

        return carry

    lax.fori_loop(0, panels + 1, tick, 0)

    def close(p, carry):
        span = pl.ds(pl.multiple_of(p * wide, wide), wide)

        @pl.when(last)
        def _():
            total = zout[p, 0]
            for dz in range(1, nz):
                last_copy(p, dz).wait_recv()
                total = total + zlast[p, dz]
            leaving_ref[:, span, :] = total
            for dz in range(1, nz):
                last_copy(p, dz).wait_send()

        @pl.when(inner)
        def _():
            back(p).wait_recv()
            leaving_ref[:, span, :] = bin_[p]
            for dz in range(nz):
                z_copy(p, dz).wait_send()

        for dz in order:
            for dx in range(1, nx):
                x_copy(p, dx, dz).wait_send()

        @pl.when(g > 0)
        def _():
            back(p).wait_send()

        return carry

    lax.fori_loop(0, panels, close, 0)


def local(nx, groups, col_devices, sources, diag_inverse, factor_tiles, tile_rows, tile_cols):
    per, panel_sources, size = sources.shape[1:]
    nz = col_devices // nx
    panels = PANELS if panel_sources % (16 * PANELS) == 0 else 1
    high, low = merge(factor_tiles[0], tile_rows, tile_cols, per * col_devices, per)
    block = (per, panel_sources, size)
    cut = (per, panel_sources // panels, size)
    whole = pl.BlockSpec(memory_space=pltpu.VMEM)
    dma = pltpu.SemaphoreType.DMA
    by_x = (panels, nx - 1, nz)
    by_z = (panels, nz)
    solved, leaving = pl.pallas_call(
        functools.partial(chain_kernel, groups, nx, nz, panels),
        out_shape=[jax.ShapeDtypeStruct(block, jnp.float32)] * 2,
        in_specs=[whole] * 4,
        out_specs=[whole] * 2,
        scratch_shapes=[
            pltpu.VMEM((per, size, size), jnp.bfloat16),
            pltpu.VMEM((per, size, size), jnp.bfloat16),
            pltpu.VMEM((2 * cut[1], per * size), jnp.bfloat16),
            pltpu.VMEM(by_z + cut, jnp.float32),
            pltpu.VMEM(by_x + cut, jnp.float32),
            pltpu.VMEM(by_x + cut, jnp.float32),
            pltpu.VMEM(by_z + cut, jnp.float32),
            pltpu.VMEM(by_z + cut, jnp.float32),
            pltpu.VMEM(by_z + cut, jnp.float32),
            pltpu.VMEM((panels,) + cut, jnp.float32),
            pltpu.VMEM((panels,) + cut, jnp.float32),
            dma(by_x),
            dma(by_x),
            dma(by_z),
            dma(by_z),
            dma(by_z),
            dma((panels,)),
            dma((panels,)),
        ],
        compiler_params=pltpu.CompilerParams(
            collective_id=0, has_side_effects=True, vmem_limit_bytes=36 * MIB
        ),
    )(sources[0], diag_inverse[0], high, low)
    return (solved[None], leaving[None])


def solution(mesh):
    groups, col_devices = mesh.shape["chain"], mesh.shape["col"]
    nx = max(d for d in range(1, col_devices + 1) if col_devices % d == 0 and d * d <= col_devices)
    return jax.shard_map(
        functools.partial(local, nx, groups, col_devices),
        mesh=mesh,
        in_specs=(
            P("chain", "col", None, None),
            P("chain", "col", None, None),
            P("chain", "col", None, None),
            P("chain", "col"),
            P("chain", "col"),
        ),
        out_specs=(P("chain", "col", None, None), P("chain", "col", None, None)),
        check_vma=False,
    )
```

time: 380 us -> 58.6 us (0.15)
  waiting for transfers between devices: 270 us -> 0 us
  matrix products: 73.3 us -> 0 us
  Pallas kernels: 0 us -> 56.5 us
  between operations: 13.7 us -> 0.68 us
  local copies, waits for them, and re-layouts: 12.7 us -> 1.32 us
  starting transfers between devices: 5.17 us -> 0 us
    reduce_scatter x4 -> x0, waiting for transfers between devices: 255 us -> none  [advance(): lax.psum_scatter(jnp.einsum('kt,ksr->tsr', onehot, products, precision=hi...]
    dot_general x12 -> x0, matrix products: 73.3 us -> none  [the longest x4 54.7 us: advance(): products = jnp.einsum('krc,ksc->ksr', factor, picked, precision=highest)]
    pallas_call x0 -> x2, Pallas kernels: none -> 56.5 us  [the longest x1 51 us: local(): pl.pallas_call(functools.partial(chain_kernel, groups, nx, nz, panels), o...]
    ppermute x4 -> x0, waiting for transfers between devices: 14.3 us -> none  [shifted(): return lax.ppermute(block, axis, route)]
    dot_general x4 -> x0, local copies, waits for them, and re-layouts: 6.31 us -> none  [advance(): jnp.einsum('kt,ksr->tsr', onehot, products, precision=highest)]
    ppermute x4 -> x0, starting transfers between devices: 5.12 us -> none  [shifted(): return lax.ppermute(block, axis, route)]
  transfers between devices with their start and end apart: 8 -> 0, of which waited for: 8 -> 0; matrix products, arithmetic and copies ran while one was open for 0% -> 0% of each run, Pallas kernels for 0% -> 0%
where the time goes in v2:
time: 58.6 us; the launch traced here: 58.5 us
  Pallas kernels  56.5 us (96%)
  local copies, waits for them, and re-layouts  1.32 us (2%)
  between operations  0.68 us (1%)
    pallas_call x1, Pallas kernels, local(): pl.pallas_call(functools.partial(chain_kernel, groups, nx, nz, panels), o...  51 us
    pallas_call x1, Pallas kernels, merge(): pl.pallas_call(functools.partial(merge_kernel, pieces), out_shape=[pltpu....  5.46 us
    unnamed x6, local copies, waits for them, and re-layouts  1.32 us

profile of v2, /device:TPU:5, one launch (start us, length us, event | category | flops | bytes accessed | tf_op | source)
XLA Modules:
  0.0 58.5 jit_solution(18027198519249131561)
XLA Ops:
  0.6 0.0 copy-start
  0.6 0.0 copy-start.1
  0.7 5.5 %shard_map.68 = (bf16[4096,512]{1,0:T(8,128)(2,1)S(1)}, bf16[4096,512]{1,0:T(8,128)(2,1)S(1)}) custom-call(s32[1,94]{1,0:T(1,128)} %rows_ref.1, s32[1,94]{1,0:T(1,128)} %cols_ref.1, f32[94,128,128]{2,1,0:T(8,128)} %bitcast.9), custom_call_target="tpu_custom_call" | custom-call | tf_op jit(solution)/shard_map/pallas_call | solution.py:72
  6.1 0.0 copy-done
  6.1 0.0 copy-done.1
  6.1 51.0 %shard_map.69 = (f32[4,64,128]{2,1,0:T(8,128)S(1)}, f32[4,64,128]{2,1,0:T(8,128)S(1)}) custom-call(f32[4,64,128]{2,1,0:T(8,128)S(1)} %bitcast.6, f32[4,128,128]{2,1,0:T(8,128)S(1)} %bitcast.5, bf16[4096,512]{1,0:T(8,128)(2,1)S(1)} %get-tuple-element.6.high_ref, bf16[4096,512]{1,0:T(8,128)(2,1)S(1)} %get-tuple-element.7.low_ref), custom_call_target="tpu_custom_call" | custom-call | tf_op jit(solution)/shard_map/pallas_call | solution.py:280
  57.2 0.7 %copy.9 = f32[1,4,64,128]{3,2,1,0:T(8,128)} copy(f32[1,4,64,128]{3,2,1,0:T(8,128)S(1)} %bitcast.8) | data formatting | bytes 262144
  57.8 0.7 %copy.10 = f32[1,4,64,128]{3,2,1,0:T(8,128)} copy(f32[1,4,64,128]{3,2,1,0:T(8,128)S(1)} %bitcast.7) | data formatting | bytes 262144
Async XLA Ops:
  0.6 5.5 %copy-start = (f32[1,4,128,128]{3,2,1,0:T(8,128)S(1)}, f32[1,4,128,128]{3,2,1,0:T(8,128)}, u32[]{:S(2)}) copy-start(f32[1,4,128,128]{3,2,1,0:T(8,128)} %param.6) | copy-start | bytes 786436
  0.6 5.5 %copy-start.1 = (f32[1,4,64,128]{3,2,1,0:T(8,128)S(1)}, f32[1,4,64,128]{3,2,1,0:T(8,128)}, u32[]{:S(2)}) copy-start(f32[1,4,64,128]{3,2,1,0:T(8,128)} %param.5) | copy-start | bytes 393220

commit v3 on v2

--- a/solution.py
+++ b/solution.py
@@ -9,7 +9,7 @@
 
 MESH = pl.DeviceIdType.MESH
 MIB = 1 << 20
-PANELS = 4
+PANELS = 2
 
 
 def split(value):
@@ -220,18 +220,12 @@
                 def _():
                     last_copy(p, dz).start()
 
-    def tick(moment, carry):
-        @pl.when(moment < panels)
-        def _():
-            first(moment)
-
-        @pl.when(moment > 0)
-        def _():
-            second(moment - 1)
-
-        return carry
-
-    lax.fori_loop(0, panels + 1, tick, 0)
+    def tick(p, carry):
+        first(p)
+        second(p)
+        return carry
+
+    lax.fori_loop(0, panels, tick, 0)
 
     def close(p, carry):
         span = pl.ds(pl.multiple_of(p * wide, wide), wide)

time: 58.6 us -> 53.4 us (0.911)
  Pallas kernels: 56.5 us -> 51.3 us
    pallas_call x1, Pallas kernels: 51 us -> 45.8 us  [local(): pl.pallas_call(functools.partial(chain_kernel, groups, nx, nz, panels), o...]
where the time goes in v3:
time: 53.4 us; the launch traced here: 53.3 us
  Pallas kernels  51.3 us (96%)
  local copies, waits for them, and re-layouts  1.32 us (2%)
  between operations  0.68 us (1%)
    pallas_call x1, Pallas kernels, local(): pl.pallas_call(functools.partial(chain_kernel, groups, nx, nz, panels), o...  45.8 us
    pallas_call x1, Pallas kernels, merge(): pl.pallas_call(functools.partial(merge_kernel, pieces), out_shape=[pltpu....  5.46 us
    unnamed x6, local copies, waits for them, and re-layouts  1.32 us

profile of v3, /device:TPU:5, one launch (start us, length us, event | category | flops | bytes accessed | tf_op | source)
XLA Modules:
  0.0 53.3 jit_solution(6250877005560583301)
XLA Ops:
  0.6 0.0 copy-start
  0.6 0.0 copy-start.1
  0.7 5.5 %shard_map.68 = (bf16[4096,512]{1,0:T(8,128)(2,1)S(1)}, bf16[4096,512]{1,0:T(8,128)(2,1)S(1)}) custom-call(s32[1,94]{1,0:T(1,128)} %rows_ref.1, s32[1,94]{1,0:T(1,128)} %cols_ref.1, f32[94,128,128]{2,1,0:T(8,128)} %bitcast.9), custom_call_target="tpu_custom_call" | custom-call | tf_op jit(solution)/shard_map/pallas_call | solution.py:72
  6.1 0.0 copy-done
  6.1 0.0 copy-done.1
  6.1 45.8 %shard_map.69 = (f32[4,64,128]{2,1,0:T(8,128)S(1)}, f32[4,64,128]{2,1,0:T(8,128)S(1)}) custom-call(f32[4,64,128]{2,1,0:T(8,128)S(1)} %bitcast.6, f32[4,128,128]{2,1,0:T(8,128)S(1)} %bitcast.5, bf16[4096,512]{1,0:T(8,128)(2,1)S(1)} %get-tuple-element.6.high_ref, bf16[4096,512]{1,0:T(8,128)(2,1)S(1)} %get-tuple-element.7.low_ref), custom_call_target="tpu_custom_call" | custom-call | tf_op jit(solution)/shard_map/pallas_call | solution.py:274
  52.0 0.7 %copy.9 = f32[1,4,64,128]{3,2,1,0:T(8,128)} copy(f32[1,4,64,128]{3,2,1,0:T(8,128)S(1)} %bitcast.8) | data formatting | bytes 262144
  52.6 0.7 %copy.10 = f32[1,4,64,128]{3,2,1,0:T(8,128)} copy(f32[1,4,64,128]{3,2,1,0:T(8,128)S(1)} %bitcast.7) | data formatting | bytes 262144
Async XLA Ops:
  0.6 5.5 %copy-start = (f32[1,4,128,128]{3,2,1,0:T(8,128)S(1)}, f32[1,4,128,128]{3,2,1,0:T(8,128)}, u32[]{:S(2)}) copy-start(f32[1,4,128,128]{3,2,1,0:T(8,128)} %param.6) | copy-start | bytes 786436
  0.6 5.5 %copy-start.1 = (f32[1,4,64,128]{3,2,1,0:T(8,128)S(1)}, f32[1,4,64,128]{3,2,1,0:T(8,128)}, u32[]{:S(2)}) copy-start(f32[1,4,64,128]{3,2,1,0:T(8,128)} %param.5) | copy-start | bytes 393220

commit v4 on v3

--- a/solution.py
+++ b/solution.py
@@ -22,10 +22,14 @@
     return lax.dot_general(left, right, (((1,), (1,)), ((), ())), preferred_element_type=jnp.float32)
 
 
-def merge_kernel(pieces, rows_ref, cols_ref, factor_ref, high_ref, low_ref, held, total, arrived):
+def times(left, right):
+    return lax.dot_general(left, right, (((1,), (0,)), ((), ())), preferred_element_type=jnp.float32)
+
+
+def merge_kernel(pieces, rows_ref, cols_ref, factor_ref, high_ref, low_ref, held, total, named, arrived):
     tiles, size, _ = factor_ref.shape
+    chunks = high_ref.shape[0]
     width = high_ref.shape[1] // size
-    blocks = high_ref.shape[0] // size
 
     def fetch(i):
         span = pl.ds(pieces[i], pieces[i + 1] - pieces[i])
@@ -34,39 +38,57 @@
     for i in range(len(pieces) - 1):
         fetch(i).start()
 
-    def clear(block, carry):
-        at = pl.ds(pl.multiple_of(block * size, size), size)
-        total[at, :] = jnp.zeros((size, total.shape[1]), jnp.float32)
-        return carry
-
-    lax.fori_loop(0, blocks, clear, 0)
+    def clear(place, carry):
+        named[place] = 0
+        return carry
+
+    lax.fori_loop(0, chunks * width * width, clear, 0)
 
     def add(k, carry):
-        row = pl.ds(pl.multiple_of(rows_ref[0, k] * size, size), size)
-        col = pl.ds(pl.multiple_of(lax.rem(cols_ref[0, k], width) * size, size), size)
-        total[row, col] += held[k]
+        place = rows_ref[0, k] * width + lax.rem(cols_ref[0, k], width)
+        fresh = named[place] == 0
+        named[place] = 1
+
+        @pl.when(fresh)
+        def _():
+            total[place] = held[k]
+
+        @pl.when(jnp.logical_not(fresh))
+        def _():
+            total[place] += held[k]
+
         return carry
 
     for i in range(len(pieces) - 1):
         fetch(i).wait()
         lax.fori_loop(pieces[i], pieces[i + 1], add, 0)
 
-    def finish(block, carry):
-        at = pl.ds(pl.multiple_of(block * size, size), size)
-        for c in range(width):
-            cs = slice(c * size, (c + 1) * size)
-            high, low = split(total[at, cs])
-            high_ref[at, cs] = high
-            low_ref[at, cs] = low
-        return carry
-
-    lax.fori_loop(0, blocks, finish, 0)
-
-
-def merge(factor, rows, cols, row_tiles, col_tiles):
+    def finish(chunk, carry):
+        for r in range(width):
+            for c in range(width):
+                place = (chunk * width + r) * width + c
+                cs, rs = slice(c * size, (c + 1) * size), slice(r * size, (r + 1) * size)
+
+                @pl.when(named[place] != 0)
+                def _():
+                    high, low = split(total[place].T)
+                    high_ref[chunk, cs, rs] = high
+                    low_ref[chunk, cs, rs] = low
+
+                @pl.when(named[place] == 0)
+                def _():
+                    high_ref[chunk, cs, rs] = jnp.zeros((size, size), jnp.bfloat16)
+                    low_ref[chunk, cs, rs] = jnp.zeros((size, size), jnp.bfloat16)
+
+        return carry
+
+    lax.fori_loop(0, chunks, finish, 0)
+
+
+def merge(factor, rows, cols, chunks, width):
     tiles, size, _ = factor.shape
     pieces = list(range(0, tiles, 16)) + [tiles]
-    shape = (row_tiles * size, col_tiles * size)
+    shape = (chunks, width * size, width * size)
     whole = pl.BlockSpec(memory_space=pltpu.VMEM)
     scalars = pl.BlockSpec(memory_space=pltpu.SMEM)
     return pl.pallas_call(
@@ -76,7 +98,8 @@
         out_specs=[whole] * 2,
         scratch_shapes=[
             pltpu.VMEM(factor.shape, jnp.float32),
-            pltpu.VMEM(shape, jnp.float32),
+            pltpu.VMEM((chunks * width * width, size, size), jnp.float32),
+            pltpu.SMEM((chunks * width * width,), jnp.int32),
             pltpu.SemaphoreType.DMA((len(pieces) - 1,)),
         ],
         compiler_params=pltpu.CompilerParams(vmem_limit_bytes=40 * MIB),
@@ -165,10 +188,9 @@
     order = sorted(range(1, nz), key=lambda d: abs(2 * d - nz)) + [0]
 
     def chunk(dx, dz):
-        rows = per * size
-        at = pl.ds(pl.multiple_of(place(dx, dz) * rows, rows), rows)
-        both = times_transposed(operand[...], high_ref[at, :])
-        return both[:wide] + both[wide:] + times_transposed(operand[:wide, :], low_ref[at, :])
+        at = place(dx, dz)
+        both = times(operand[...], high_ref[at])
+        return both[:wide] + both[wide:] + times(operand[:wide, :], low_ref[at])
 
     def first(p):
         @pl.when(g > 0)
@@ -264,7 +286,7 @@
     per, panel_sources, size = sources.shape[1:]
     nz = col_devices // nx
     panels = PANELS if panel_sources % (16 * PANELS) == 0 else 1
-    high, low = merge(factor_tiles[0], tile_rows, tile_cols, per * col_devices, per)
+    high, low = merge(factor_tiles[0], tile_rows, tile_cols, col_devices, per)
     block = (per, panel_sources, size)
     cut = (per, panel_sources // panels, size)
     whole = pl.BlockSpec(memory_space=pltpu.VMEM)

time: 53.4 us -> 61 us (1.14)
  Pallas kernels: 51.3 us -> 58.8 us
    pallas_call x1, Pallas kernels: 5.46 us -> 13.3 us  [merge(): pl.pallas_call(functools.partial(merge_kernel, pieces), out_shape=[pltpu....]
where the time goes in v4:
time: 61 us; the launch traced here: 60.8 us
  Pallas kernels  58.8 us (96%)
  local copies, waits for them, and re-layouts  1.32 us (2%)
  between operations  0.68 us (1%)
    pallas_call x1, Pallas kernels, local(): pl.pallas_call(functools.partial(chain_kernel, groups, nx, nz, panels), o...  45.6 us
    pallas_call x1, Pallas kernels, merge(): pl.pallas_call(functools.partial(merge_kernel, pieces), out_shape=[pltpu....  13.3 us
    unnamed x6, local copies, waits for them, and re-layouts  1.32 us

profile of v4, /device:TPU:5, one launch (start us, length us, event | category | flops | bytes accessed | tf_op | source)
XLA Modules:
  0.0 60.8 jit_solution(1675149454609648600)
XLA Ops:
  0.6 0.0 copy-start
  0.6 0.0 copy-start.1
  0.7 13.3 %shard_map.68 = (bf16[8,512,512]{2,1,0:T(8,128)(2,1)S(1)}, bf16[8,512,512]{2,1,0:T(8,128)(2,1)S(1)}) custom-call(s32[1,94]{1,0:T(1,128)} %rows_ref.1, s32[1,94]{1,0:T(1,128)} %cols_ref.1, f32[94,128,128]{2,1,0:T(8,128)} %bitcast.9), custom_call_target="tpu_custom_call" | custom-call | tf_op jit(solution)/shard_map/pallas_call | solution.py:94
  13.9 0.0 copy-done
  13.9 0.0 copy-done.1
  13.9 45.6 %shard_map.69 = (f32[4,64,128]{2,1,0:T(8,128)S(1)}, f32[4,64,128]{2,1,0:T(8,128)S(1)}) custom-call(f32[4,64,128]{2,1,0:T(8,128)S(1)} %bitcast.6, f32[4,128,128]{2,1,0:T(8,128)S(1)} %bitcast.5, bf16[8,512,512]{2,1,0:T(8,128)(2,1)S(1)} %get-tuple-element.6.high_ref, bf16[8,512,512]{2,1,0:T(8,128)(2,1)S(1)} %get-tuple-element.7.low_ref), custom_call_target="tpu_custom_call" | custom-call | tf_op jit(solution)/shard_map/pallas_call | solution.py:296
  59.5 0.7 %copy.9 = f32[1,4,64,128]{3,2,1,0:T(8,128)} copy(f32[1,4,64,128]{3,2,1,0:T(8,128)S(1)} %bitcast.8) | data formatting | bytes 262144
  60.2 0.7 %copy.10 = f32[1,4,64,128]{3,2,1,0:T(8,128)} copy(f32[1,4,64,128]{3,2,1,0:T(8,128)S(1)} %bitcast.7) | data formatting | bytes 262144
Async XLA Ops:
  0.6 13.3 %copy-start = (f32[1,4,128,128]{3,2,1,0:T(8,128)S(1)}, f32[1,4,128,128]{3,2,1,0:T(8,128)}, u32[]{:S(2)}) copy-start(f32[1,4,128,128]{3,2,1,0:T(8,128)} %param.6) | copy-start | bytes 786436
  0.6 13.3 %copy-start.1 = (f32[1,4,64,128]{3,2,1,0:T(8,128)S(1)}, f32[1,4,64,128]{3,2,1,0:T(8,128)}, u32[]{:S(2)}) copy-start(f32[1,4,64,128]{3,2,1,0:T(8,128)} %param.5) | copy-start | bytes 393220

commit v5 on v3

--- a/solution.py
+++ b/solution.py
@@ -86,8 +86,8 @@
 def chain_kernel(
     groups, nx, nz, panels,
     src_ref, inv_ref, high_ref, low_ref, solved_ref, leaving_ref,
-    inv_high, inv_low, operand, own, xout, xin, zout, zin, zlast, bout, bin_,
-    xsend, xrecv, zsend, zrecv, lrecv, bsend, brecv,
+    inv_high, inv_low, operand, xout, xin, zout, zin, zlast, bout, bin_, whole, fed_in,
+    xsend, xrecv, zsend, zrecv, lrecv, bsend, brecv, fsend, frecv,
 ):
     g = lax.axis_index("chain")
     col = lax.axis_index("col")
@@ -96,7 +96,12 @@
     per, sources, size = src_ref.shape
     wide = sources // panels
     last = g == groups - 1
-    inner = jnp.logical_not(last)
+    odd = lax.rem(g, 2) == 1
+    even = jnp.logical_not(odd)
+    keeps = odd | last
+    near = jnp.logical_not(keeps)
+    far = odd & jnp.logical_not(last)
+    fed = even & (g > 0)
 
     def place(dx, dz):
         return lax.rem(z + dz, nz) * nx + lax.rem(x + dx, nx)
@@ -109,21 +114,29 @@
     for dx in range(1, nx):
         greet(g, dx, 0)
 
-    @pl.when(g > 0)
+    @pl.when(odd)
     def _():
         for dz in range(nz):
             greet(g - 1, 0, dz)
 
-    @pl.when(inner)
+    @pl.when(near)
     def _():
         for dz in range(nz):
             greet(g + 1, 0, dz)
 
-    @pl.when(last)
+    @pl.when(keeps)
     def _():
         for dz in range(1, nz):
             greet(g, 0, dz)
 
+    @pl.when(far)
+    def _():
+        greet(g + 1, 0, 0)
+
+    @pl.when(fed)
+    def _():
+        greet(g - 1, 0, 0)
+
     for t in range(per):
         inv_high[t], inv_low[t] = split(inv_ref[t])
 
@@ -131,7 +144,10 @@
     def _():
         bout[...] = jnp.zeros(bout.shape, jnp.float32)
 
-    awaited = (nx - 1) + jnp.where(g > 0, nz, 0) + jnp.where(last, nz - 1, nz)
+    awaited = (
+        (nx - 1) + jnp.where(odd, nz, 0) + jnp.where(keeps, nz - 1, nz)
+        + jnp.where(far, 1, 0) + jnp.where(fed, 1, 0)
+    )
     pl.semaphore_wait(barrier, awaited)
 
     def x_copy(p, dx, dz):
@@ -160,6 +176,13 @@
             src_ref=bout.at[p], dst_ref=bin_.at[p],
             send_sem=bsend.at[p], recv_sem=brecv.at[p],
             device_id=(g - 1, col), device_id_type=MESH,
+        )
+
+    def forward(p):
+        return pltpu.make_async_remote_copy(
+            src_ref=whole.at[p], dst_ref=fed_in.at[p],
+            send_sem=fsend.at[p], recv_sem=frecv.at[p],
+            device_id=(g + 1, col), device_id_type=MESH,
         )
 
     order = sorted(range(1, nz), key=lambda d: abs(2 * d - nz)) + [0]
@@ -171,7 +194,7 @@
         return both[:wide] + both[wide:] + times_transposed(operand[:wide, :], low_ref[at, :])
 
     def first(p):
-        @pl.when(g > 0)
+        @pl.when(odd)
         def _():
             for dz in range(nz):
                 z_copy(p, dz).wait_recv()
@@ -180,6 +203,11 @@
                 total = total + zin[p, dz]
             bout[p] = total
             back(p).start()
+
+        @pl.when(fed)
+        def _():
+            forward(p).wait_recv()
+            bout[p] = fed_in[p]
 
         span = pl.ds(pl.multiple_of(p * wide, wide), wide)
         for t in range(per):
@@ -197,32 +225,43 @@
                 for t in range(per):
                     xout[p, dx - 1, dz, t] = result[:, t * size:(t + 1) * size]
                 x_copy(p, dx, dz).start()
+
+    def second(p):
         for dz in order:
             result = chunk(0, dz)
-            for t in range(per):
-                own[p, dz, t] = result[:, t * size:(t + 1) * size]
-
-    def second(p):
-        for dz in order:
             for dx in range(1, nx):
                 x_copy(p, dx, dz).wait_recv()
-            part = own[p, dz]
-            for dx in range(1, nx):
-                part = part + xin[p, dx - 1, dz]
-            zout[p, dz] = part
-
-            @pl.when(inner)
+            for t in range(per):
+                part = result[:, t * size:(t + 1) * size]
+                for dx in range(1, nx):
+                    part = part + xin[p, dx - 1, dz, t]
+                zout[p, dz, t] = part
+
+            @pl.when(near)
             def _():
                 z_copy(p, dz).start()
 
             if dz > 0:
-                @pl.when(last)
+                @pl.when(keeps)
                 def _():
                     last_copy(p, dz).start()
+
+    def gather(p):
+        total = zout[p, 0]
+        for dz in range(1, nz):
+            last_copy(p, dz).wait_recv()
+            total = total + zlast[p, dz]
+        whole[p] = total
 
     def tick(p, carry):
         first(p)
         second(p)
+
+        @pl.when(far)
+        def _():
+            gather(p)
+            forward(p).start()
+
         return carry
 
     lax.fori_loop(0, panels, tick, 0)
@@ -232,15 +271,19 @@
 
         @pl.when(last)
         def _():
-            total = zout[p, 0]
-            for dz in range(1, nz):
-                last_copy(p, dz).wait_recv()
-                total = total + zlast[p, dz]
-            leaving_ref[:, span, :] = total
+            gather(p)
+
+        @pl.when(keeps)
+        def _():
+            leaving_ref[:, span, :] = whole[p]
             for dz in range(1, nz):
                 last_copy(p, dz).wait_send()
 
-        @pl.when(inner)
+        @pl.when(far)
+        def _():
+            forward(p).wait_send()
+
+        @pl.when(near)
         def _():
             back(p).wait_recv()
             leaving_ref[:, span, :] = bin_[p]
@@ -251,7 +294,7 @@
             for dx in range(1, nx):
                 x_copy(p, dx, dz).wait_send()
 
-        @pl.when(g > 0)
+        @pl.when(odd)
         def _():
             back(p).wait_send()
 
@@ -280,7 +323,6 @@
             pltpu.VMEM((per, size, size), jnp.bfloat16),
             pltpu.VMEM((per, size, size), jnp.bfloat16),
             pltpu.VMEM((2 * cut[1], per * size), jnp.bfloat16),
-            pltpu.VMEM(by_z + cut, jnp.float32),
             pltpu.VMEM(by_x + cut, jnp.float32),
             pltpu.VMEM(by_x + cut, jnp.float32),
             pltpu.VMEM(by_z + cut, jnp.float32),
@@ -288,11 +330,15 @@
             pltpu.VMEM(by_z + cut, jnp.float32),
             pltpu.VMEM((panels,) + cut, jnp.float32),
             pltpu.VMEM((panels,) + cut, jnp.float32),
+            pltpu.VMEM((panels,) + cut, jnp.float32),
+            pltpu.VMEM((panels,) + cut, jnp.float32),
             dma(by_x),
             dma(by_x),
             dma(by_z),
             dma(by_z),
             dma(by_z),
+            dma((panels,)),
+            dma((panels,)),
             dma((panels,)),
             dma((panels,)),
         ],

time: 53.4 us -> 57.7 us (1.081)
  Pallas kernels: 51.3 us -> 55.5 us
    pallas_call x1, Pallas kernels: 45.8 us -> 50 us  [local(): pl.pallas_call(functools.partial(chain_kernel, groups, nx, nz, panels), o...]
where the time goes in v5:
time: 57.7 us; the launch traced here: 57.5 us
  Pallas kernels  55.5 us (96%)
  local copies, waits for them, and re-layouts  1.32 us (2%)
  between operations  0.68 us (1%)
    pallas_call x1, Pallas kernels, local(): pl.pallas_call(functools.partial(chain_kernel, groups, nx, nz, panels), o...  50 us
    pallas_call x1, Pallas kernels, merge(): pl.pallas_call(functools.partial(merge_kernel, pieces), out_shape=[pltpu....  5.46 us
    unnamed x6, local copies, waits for them, and re-layouts  1.32 us

profile of v5, /device:TPU:5, one launch (start us, length us, event | category | flops | bytes accessed | tf_op | source)
XLA Modules:
  0.0 57.5 jit_solution(14467667566795101564)
XLA Ops:
  0.6 0.0 copy-start
  0.6 0.0 copy-start.1
  0.7 5.5 %shard_map.68 = (bf16[4096,512]{1,0:T(8,128)(2,1)S(1)}, bf16[4096,512]{1,0:T(8,128)(2,1)S(1)}) custom-call(s32[1,94]{1,0:T(1,128)} %rows_ref.1, s32[1,94]{1,0:T(1,128)} %cols_ref.1, f32[94,128,128]{2,1,0:T(8,128)} %bitcast.9), custom_call_target="tpu_custom_call" | custom-call | tf_op jit(solution)/shard_map/pallas_call | solution.py:72
  6.1 0.0 copy-done
  6.1 0.0 copy-done.1
  6.1 50.0 %shard_map.69 = (f32[4,64,128]{2,1,0:T(8,128)S(1)}, f32[4,64,128]{2,1,0:T(8,128)S(1)}) custom-call(f32[4,64,128]{2,1,0:T(8,128)S(1)} %bitcast.6, f32[4,128,128]{2,1,0:T(8,128)S(1)} %bitcast.5, bf16[4096,512]{1,0:T(8,128)(2,1)S(1)} %get-tuple-element.6.high_ref, bf16[4096,512]{1,0:T(8,128)(2,1)S(1)} %get-tuple-element.7.low_ref), custom_call_target="tpu_custom_call" | custom-call | tf_op jit(solution)/shard_map/pallas_call | solution.py:317
  56.2 0.7 %copy.9 = f32[1,4,64,128]{3,2,1,0:T(8,128)} copy(f32[1,4,64,128]{3,2,1,0:T(8,128)S(1)} %bitcast.8) | data formatting | bytes 262144
  56.9 0.7 %copy.10 = f32[1,4,64,128]{3,2,1,0:T(8,128)} copy(f32[1,4,64,128]{3,2,1,0:T(8,128)S(1)} %bitcast.7) | data formatting | bytes 262144
Async XLA Ops:
  0.6 5.5 %copy-start = (f32[1,4,128,128]{3,2,1,0:T(8,128)S(1)}, f32[1,4,128,128]{3,2,1,0:T(8,128)}, u32[]{:S(2)}) copy-start(f32[1,4,128,128]{3,2,1,0:T(8,128)} %param.6) | copy-start | bytes 786436
  0.6 5.5 %copy-start.1 = (f32[1,4,64,128]{3,2,1,0:T(8,128)S(1)}, f32[1,4,64,128]{3,2,1,0:T(8,128)}, u32[]{:S(2)}) copy-start(f32[1,4,64,128]{3,2,1,0:T(8,128)} %param.5) | copy-start | bytes 393220

commit v6 on v5

--- a/solution.py
+++ b/solution.py
@@ -86,7 +86,7 @@
 def chain_kernel(
     groups, nx, nz, panels,
     src_ref, inv_ref, high_ref, low_ref, solved_ref, leaving_ref,
-    inv_high, inv_low, operand, xout, xin, zout, zin, zlast, bout, bin_, whole, fed_in,
+    inv_high, inv_low, operand, own, xout, xin, zout, zin, zlast, bout, bin_, whole, fed_in,
     xsend, xrecv, zsend, zrecv, lrecv, bsend, brecv, fsend, frecv,
 ):
     g = lax.axis_index("chain")
@@ -193,6 +193,12 @@
         both = times_transposed(operand[...], high_ref[at, :])
         return both[:wide] + both[wide:] + times_transposed(operand[:wide, :], low_ref[at, :])
 
+    def fill(dx, store):
+        results = [chunk(dx, dz) for dz in order]
+        for dz, result in zip(order, results):
+            for t in range(per):
+                store[dz, t] = result[:, t * size:(t + 1) * size]
+
     def first(p):
         @pl.when(odd)
         def _():
@@ -219,23 +225,20 @@
             operand[:wide, t * size:(t + 1) * size] = high
             operand[wide:, t * size:(t + 1) * size] = low
 
+        for dx in range(1, nx):
+            fill(dx, xout.at[p, dx - 1])
+            for dz in order:
+                x_copy(p, dx, dz).start()
+        fill(0, own.at[p])
+
+    def second(p):
         for dz in order:
             for dx in range(1, nx):
-                result = chunk(dx, dz)
-                for t in range(per):
-                    xout[p, dx - 1, dz, t] = result[:, t * size:(t + 1) * size]
-                x_copy(p, dx, dz).start()
-
-    def second(p):
-        for dz in order:
-            result = chunk(0, dz)
+                x_copy(p, dx, dz).wait_recv()
+            part = own[p, dz]
             for dx in range(1, nx):
-                x_copy(p, dx, dz).wait_recv()
-            for t in range(per):
-                part = result[:, t * size:(t + 1) * size]
-                for dx in range(1, nx):
-                    part = part + xin[p, dx - 1, dz, t]
-                zout[p, dz, t] = part
+                part = part + xin[p, dx - 1, dz]
+            zout[p, dz] = part
 
             @pl.when(near)
             def _():
@@ -323,6 +326,7 @@
             pltpu.VMEM((per, size, size), jnp.bfloat16),
             pltpu.VMEM((per, size, size), jnp.bfloat16),
             pltpu.VMEM((2 * cut[1], per * size), jnp.bfloat16),
+            pltpu.VMEM(by_z + cut, jnp.float32),
             pltpu.VMEM(by_x + cut, jnp.float32),
             pltpu.VMEM(by_x + cut, jnp.float32),
             pltpu.VMEM(by_z + cut, jnp.float32),

time: 57.7 us -> 62.4 us (1.081)
  Pallas kernels: 55.5 us -> 60.2 us
    pallas_call x1, Pallas kernels: 50 us -> 54.7 us  [local(): pl.pallas_call(functools.partial(chain_kernel, groups, nx, nz, panels), o...]
where the time goes in v6:
time: 62.4 us; the launch traced here: 62.2 us
  Pallas kernels  60.2 us (96%)
  local copies, waits for them, and re-layouts  1.32 us (2%)
  between operations  0.68 us (1%)
    pallas_call x1, Pallas kernels, local(): pl.pallas_call(functools.partial(chain_kernel, groups, nx, nz, panels), o...  54.7 us
    pallas_call x1, Pallas kernels, merge(): pl.pallas_call(functools.partial(merge_kernel, pieces), out_shape=[pltpu....  5.46 us
    unnamed x6, local copies, waits for them, and re-layouts  1.32 us

profile of v6, /device:TPU:5, one launch (start us, length us, event | category | flops | bytes accessed | tf_op | source)
XLA Modules:
  0.0 62.2 jit_solution(13499437854834280513)
XLA Ops:
  0.6 0.0 copy-start
  0.6 0.0 copy-start.1
  0.7 5.5 %shard_map.68 = (bf16[4096,512]{1,0:T(8,128)(2,1)S(1)}, bf16[4096,512]{1,0:T(8,128)(2,1)S(1)}) custom-call(s32[1,94]{1,0:T(1,128)} %rows_ref.1, s32[1,94]{1,0:T(1,128)} %cols_ref.1, f32[94,128,128]{2,1,0:T(8,128)} %bitcast.9), custom_call_target="tpu_custom_call" | custom-call | tf_op jit(solution)/shard_map/pallas_call | solution.py:72
  6.1 0.0 copy-done
  6.1 0.0 copy-done.1
  6.1 54.7 %shard_map.69 = (f32[4,64,128]{2,1,0:T(8,128)S(1)}, f32[4,64,128]{2,1,0:T(8,128)S(1)}) custom-call(f32[4,64,128]{2,1,0:T(8,128)S(1)} %bitcast.6, f32[4,128,128]{2,1,0:T(8,128)S(1)} %bitcast.5, bf16[4096,512]{1,0:T(8,128)(2,1)S(1)} %get-tuple-element.6.high_ref, bf16[4096,512]{1,0:T(8,128)(2,1)S(1)} %get-tuple-element.7.low_ref), custom_call_target="tpu_custom_call" | custom-call | tf_op jit(solution)/shard_map/pallas_call | solution.py:320
  60.9 0.7 %copy.9 = f32[1,4,64,128]{3,2,1,0:T(8,128)} copy(f32[1,4,64,128]{3,2,1,0:T(8,128)S(1)} %bitcast.8) | data formatting | bytes 262144
  61.5 0.7 %copy.10 = f32[1,4,64,128]{3,2,1,0:T(8,128)} copy(f32[1,4,64,128]{3,2,1,0:T(8,128)S(1)} %bitcast.7) | data formatting | bytes 262144
Async XLA Ops:
  0.6 5.5 %copy-start = (f32[1,4,128,128]{3,2,1,0:T(8,128)S(1)}, f32[1,4,128,128]{3,2,1,0:T(8,128)}, u32[]{:S(2)}) copy-start(f32[1,4,128,128]{3,2,1,0:T(8,128)} %param.6) | copy-start | bytes 786436
  0.6 5.5 %copy-start.1 = (f32[1,4,64,128]{3,2,1,0:T(8,128)S(1)}, f32[1,4,64,128]{3,2,1,0:T(8,128)}, u32[]{:S(2)}) copy-start(f32[1,4,64,128]{3,2,1,0:T(8,128)} %param.5) | copy-start | bytes 393220

commit v7 on v6

--- a/solution.py
+++ b/solution.py
@@ -193,11 +193,10 @@
         both = times_transposed(operand[...], high_ref[at, :])
         return both[:wide] + both[wide:] + times_transposed(operand[:wide, :], low_ref[at, :])
 
-    def fill(dx, store):
-        results = [chunk(dx, dz) for dz in order]
-        for dz, result in zip(order, results):
-            for t in range(per):
-                store[dz, t] = result[:, t * size:(t + 1) * size]
+    def fill(dx, dz, store):
+        result = chunk(dx, dz)
+        for t in range(per):
+            store[t] = result[:, t * size:(t + 1) * size]
 
     def first(p):
         @pl.when(odd)
@@ -225,11 +224,12 @@
             operand[:wide, t * size:(t + 1) * size] = high
             operand[wide:, t * size:(t + 1) * size] = low
 
-        for dx in range(1, nx):
-            fill(dx, xout.at[p, dx - 1])
-            for dz in order:
+        for dz in order:
+            for dx in range(1, nx):
+                fill(dx, dz, xout.at[p, dx - 1, dz])
                 x_copy(p, dx, dz).start()
-        fill(0, own.at[p])
+        for dz in order:
+            fill(0, dz, own.at[p, dz])
 
     def second(p):
         for dz in order:

time: 62.4 us -> 58.9 us (0.944)
  Pallas kernels: 60.2 us -> 56.8 us
    pallas_call x1, Pallas kernels: 54.7 us -> 51.3 us  [local(): pl.pallas_call(functools.partial(chain_kernel, groups, nx, nz, panels), o...]
where the time goes in v7:
time: 58.9 us; the launch traced here: 58.8 us
  Pallas kernels  56.8 us (96%)
  local copies, waits for them, and re-layouts  1.32 us (2%)
  between operations  0.68 us (1%)
    pallas_call x1, Pallas kernels, local(): pl.pallas_call(functools.partial(chain_kernel, groups, nx, nz, panels), o...  51.3 us
    pallas_call x1, Pallas kernels, merge(): pl.pallas_call(functools.partial(merge_kernel, pieces), out_shape=[pltpu....  5.46 us
    unnamed x6, local copies, waits for them, and re-layouts  1.32 us

profile of v7, /device:TPU:5, one launch (start us, length us, event | category | flops | bytes accessed | tf_op | source)
XLA Modules:
  0.0 58.8 jit_solution(8979624112720230986)
XLA Ops:
  0.6 0.0 copy-start
  0.6 0.0 copy-start.1
  0.7 5.5 %shard_map.68 = (bf16[4096,512]{1,0:T(8,128)(2,1)S(1)}, bf16[4096,512]{1,0:T(8,128)(2,1)S(1)}) custom-call(s32[1,94]{1,0:T(1,128)} %rows_ref.1, s32[1,94]{1,0:T(1,128)} %cols_ref.1, f32[94,128,128]{2,1,0:T(8,128)} %bitcast.9), custom_call_target="tpu_custom_call" | custom-call | tf_op jit(solution)/shard_map/pallas_call | solution.py:72
  6.1 0.0 copy-done
  6.1 0.0 copy-done.1
  6.1 51.3 %shard_map.69 = (f32[4,64,128]{2,1,0:T(8,128)S(1)}, f32[4,64,128]{2,1,0:T(8,128)S(1)}) custom-call(f32[4,64,128]{2,1,0:T(8,128)S(1)} %bitcast.6, f32[4,128,128]{2,1,0:T(8,128)S(1)} %bitcast.5, bf16[4096,512]{1,0:T(8,128)(2,1)S(1)} %get-tuple-element.6.high_ref, bf16[4096,512]{1,0:T(8,128)(2,1)S(1)} %get-tuple-element.7.low_ref), custom_call_target="tpu_custom_call" | custom-call | tf_op jit(solution)/shard_map/pallas_call | solution.py:320
  57.5 0.7 %copy.9 = f32[1,4,64,128]{3,2,1,0:T(8,128)} copy(f32[1,4,64,128]{3,2,1,0:T(8,128)S(1)} %bitcast.8) | data formatting | bytes 262144
  58.1 0.7 %copy.10 = f32[1,4,64,128]{3,2,1,0:T(8,128)} copy(f32[1,4,64,128]{3,2,1,0:T(8,128)S(1)} %bitcast.7) | data formatting | bytes 262144
Async XLA Ops:
  0.6 5.5 %copy-start = (f32[1,4,128,128]{3,2,1,0:T(8,128)S(1)}, f32[1,4,128,128]{3,2,1,0:T(8,128)}, u32[]{:S(2)}) copy-start(f32[1,4,128,128]{3,2,1,0:T(8,128)} %param.6) | copy-start | bytes 786436
  0.6 5.5 %copy-start.1 = (f32[1,4,64,128]{3,2,1,0:T(8,128)S(1)}, f32[1,4,64,128]{3,2,1,0:T(8,128)}, u32[]{:S(2)}) copy-start(f32[1,4,64,128]{3,2,1,0:T(8,128)} %param.5) | copy-start | bytes 393220

commit v8 on v3

--- a/solution.py
+++ b/solution.py
@@ -22,10 +22,10 @@
     return lax.dot_general(left, right, (((1,), (1,)), ((), ())), preferred_element_type=jnp.float32)
 
 
-def merge_kernel(pieces, rows_ref, cols_ref, factor_ref, high_ref, low_ref, held, total, arrived):
+def merge_kernel(pieces, rows_ref, cols_ref, factor_ref, total, held, arrived):
     tiles, size, _ = factor_ref.shape
-    width = high_ref.shape[1] // size
-    blocks = high_ref.shape[0] // size
+    width = total.shape[1] // size
+    blocks = total.shape[0] // size
 
     def fetch(i):
         span = pl.ds(pieces[i], pieces[i + 1] - pieces[i])
@@ -50,17 +50,6 @@
     for i in range(len(pieces) - 1):
         fetch(i).wait()
         lax.fori_loop(pieces[i], pieces[i + 1], add, 0)
-
-    def finish(block, carry):
-        at = pl.ds(pl.multiple_of(block * size, size), size)
-        for c in range(width):
-            cs = slice(c * size, (c + 1) * size)
-            high, low = split(total[at, cs])
-            high_ref[at, cs] = high
-            low_ref[at, cs] = low
-        return carry
-
-    lax.fori_loop(0, blocks, finish, 0)
 
 
 def merge(factor, rows, cols, row_tiles, col_tiles):
@@ -71,22 +60,21 @@
     scalars = pl.BlockSpec(memory_space=pltpu.SMEM)
     return pl.pallas_call(
         functools.partial(merge_kernel, pieces),
-        out_shape=[pltpu.VMEM(shape, jnp.bfloat16)] * 2,
+        out_shape=pltpu.VMEM(shape, jnp.float32),
         in_specs=[scalars, scalars, pl.BlockSpec(memory_space=pltpu.HBM)],
-        out_specs=[whole] * 2,
+        out_specs=whole,
         scratch_shapes=[
             pltpu.VMEM(factor.shape, jnp.float32),
-            pltpu.VMEM(shape, jnp.float32),
             pltpu.SemaphoreType.DMA((len(pieces) - 1,)),
         ],
-        compiler_params=pltpu.CompilerParams(vmem_limit_bytes=40 * MIB),
+        compiler_params=pltpu.CompilerParams(vmem_limit_bytes=24 * MIB),
     )(*(pltpu.with_memory_space_constraint(a, pltpu.HBM) for a in (rows, cols, factor)))
 
 
 def chain_kernel(
     groups, nx, nz, panels,
-    src_ref, inv_ref, high_ref, low_ref, solved_ref, leaving_ref,
-    inv_high, inv_low, operand, own, xout, xin, zout, zin, zlast, bout, bin_,
+    src_ref, inv_ref, full_ref, solved_ref, leaving_ref,
+    high_ref, low_ref, inv_high, inv_low, operand, own, xout, xin, zout, zin, zlast, bout, bin_,
     xsend, xrecv, zsend, zrecv, lrecv, bsend, brecv,
 ):
     g = lax.axis_index("chain")
@@ -131,8 +119,22 @@
     def _():
         bout[...] = jnp.zeros(bout.shape, jnp.float32)
 
+    def cut_chunk(chunk_no):
+        for t in range(per):
+            at = pl.ds(pl.multiple_of((chunk_no * per + t) * size, size), size)
+            high_ref[at, :], low_ref[at, :] = split(full_ref[at, :])
+
     awaited = (nx - 1) + jnp.where(g > 0, nz, 0) + jnp.where(last, nz - 1, nz)
-    pl.semaphore_wait(barrier, awaited)
+
+    @pl.when(g > 0)
+    def _():
+        pl.semaphore_wait(barrier, awaited)
+
+        def prepare(chunk_no, carry):
+            cut_chunk(chunk_no)
+            return carry
+
+        lax.fori_loop(0, nx * nz, prepare, 0)
 
     def x_copy(p, dx, dz):
         return pltpu.make_async_remote_copy(
@@ -169,6 +171,11 @@
         at = pl.ds(pl.multiple_of(place(dx, dz) * rows, rows), rows)
         both = times_transposed(operand[...], high_ref[at, :])
         return both[:wide] + both[wide:] + times_transposed(operand[:wide, :], low_ref[at, :])
+
+    def early(p, dx, dz):
+        @pl.when((g == 0) & (p == 0))
+        def _():
+            cut_chunk(place(dx, dz))
 
     def first(p):
         @pl.when(g > 0)
@@ -193,11 +200,18 @@
 
         for dz in order:
             for dx in range(1, nx):
+                early(p, dx, dz)
                 result = chunk(dx, dz)
                 for t in range(per):
                     xout[p, dx - 1, dz, t] = result[:, t * size:(t + 1) * size]
+                if dz == order[0] and dx == 1:
+                    @pl.when((g == 0) & (p == 0))
+                    def _():
+                        pl.semaphore_wait(barrier, awaited)
+
                 x_copy(p, dx, dz).start()
         for dz in order:
+            early(p, 0, dz)
             result = chunk(0, dz)
             for t in range(per):
                 own[p, dz, t] = result[:, t * size:(t + 1) * size]
@@ -264,7 +278,7 @@
     per, panel_sources, size = sources.shape[1:]
     nz = col_devices // nx
     panels = PANELS if panel_sources % (16 * PANELS) == 0 else 1
-    high, low = merge(factor_tiles[0], tile_rows, tile_cols, per * col_devices, per)
+    full = merge(factor_tiles[0], tile_rows, tile_cols, per * col_devices, per)
     block = (per, panel_sources, size)
     cut = (per, panel_sources // panels, size)
     whole = pl.BlockSpec(memory_space=pltpu.VMEM)
@@ -274,9 +288,11 @@
     solved, leaving = pl.pallas_call(
         functools.partial(chain_kernel, groups, nx, nz, panels),
         out_shape=[jax.ShapeDtypeStruct(block, jnp.float32)] * 2,
-        in_specs=[whole] * 4,
+        in_specs=[whole] * 3,
         out_specs=[whole] * 2,
         scratch_shapes=[
+            pltpu.VMEM(full.shape, jnp.bfloat16),
+            pltpu.VMEM(full.shape, jnp.bfloat16),
             pltpu.VMEM((per, size, size), jnp.bfloat16),
             pltpu.VMEM((per, size, size), jnp.bfloat16),
             pltpu.VMEM((2 * cut[1], per * size), jnp.bfloat16),
@@ -299,7 +315,7 @@
         compiler_params=pltpu.CompilerParams(
             collective_id=0, has_side_effects=True, vmem_limit_bytes=36 * MIB
         ),
-    )(sources[0], diag_inverse[0], high, low)
+    )(sources[0], diag_inverse[0], full)
     return (solved[None], leaving[None])
 
 

time: 53.4 us -> 52.4 us (0.981)
  Pallas kernels: 51.3 us -> 50.3 us
    pallas_call x1, Pallas kernels: 5.46 us -> 3.9 us  [merge(): pl.pallas_call(functools.partial(merge_kernel, pieces), out_shape=pltpu.V...]
    pallas_call x1, Pallas kernels: 45.8 us -> 46.4 us  [local(): pl.pallas_call(functools.partial(chain_kernel, groups, nx, nz, panels), o...]
where the time goes in v8:
time: 52.4 us; the launch traced here: 52.3 us
  Pallas kernels  50.3 us (96%)
  local copies, waits for them, and re-layouts  1.32 us (3%)
  between operations  0.68 us (1%)
    pallas_call x1, Pallas kernels, local(): pl.pallas_call(functools.partial(chain_kernel, groups, nx, nz, panels), o...  46.4 us
    pallas_call x1, Pallas kernels, merge(): pl.pallas_call(functools.partial(merge_kernel, pieces), out_shape=pltpu.V...  3.9 us
    unnamed x6, local copies, waits for them, and re-layouts  1.32 us

profile of v8, /device:TPU:5, one launch (start us, length us, event | category | flops | bytes accessed | tf_op | source)
XLA Modules:
  0.0 52.3 jit_solution(4063345066946528955)
XLA Ops:
  0.6 0.0 copy-start
  0.6 0.0 copy-start.1
  0.7 3.9 %shard_map.68.full_ref = f32[4096,512]{1,0:T(8,128)S(1)} custom-call(s32[1,94]{1,0:T(1,128)} %rows_ref.1, s32[1,94]{1,0:T(1,128)} %cols_ref.1, f32[94,128,128]{2,1,0:T(8,128)} %bitcast.9), custom_call_target="tpu_custom_call" | custom-call | tf_op jit(solution)/shard_map/pallas_call | solution.py:61
  4.6 0.0 copy-done
  4.6 0.0 copy-done.1
  4.6 46.4 %shard_map.69 = (f32[4,64,128]{2,1,0:T(8,128)S(1)}, f32[4,64,128]{2,1,0:T(8,128)S(1)}) custom-call(f32[4,64,128]{2,1,0:T(8,128)S(1)} %bitcast.6, f32[4,128,128]{2,1,0:T(8,128)S(1)} %bitcast.5, f32[4096,512]{1,0:T(8,128)S(1)} %shard_map.68.full_ref), custom_call_target="tpu_custom_call" | custom-call | tf_op jit(solution)/shard_map/pallas_call | solution.py:288
  51.0 0.7 %copy.9 = f32[1,4,64,128]{3,2,1,0:T(8,128)} copy(f32[1,4,64,128]{3,2,1,0:T(8,128)S(1)} %bitcast.8) | data formatting | bytes 262144
  51.6 0.7 %copy.10 = f32[1,4,64,128]{3,2,1,0:T(8,128)} copy(f32[1,4,64,128]{3,2,1,0:T(8,128)S(1)} %bitcast.7) | data formatting | bytes 262144
Async XLA Ops:
  0.6 3.9 %copy-start = (f32[1,4,128,128]{3,2,1,0:T(8,128)S(1)}, f32[1,4,128,128]{3,2,1,0:T(8,128)}, u32[]{:S(2)}) copy-start(f32[1,4,128,128]{3,2,1,0:T(8,128)} %param.6) | copy-start | bytes 786436
  0.6 3.9 %copy-start.1 = (f32[1,4,64,128]{3,2,1,0:T(8,128)S(1)}, f32[1,4,64,128]{3,2,1,0:T(8,128)}, u32[]{:S(2)}) copy-start(f32[1,4,64,128]{3,2,1,0:T(8,128)} %param.5) | copy-start | bytes 393220

commit v9 on v8

--- a/solution.py
+++ b/solution.py
@@ -27,6 +27,8 @@
     width = total.shape[1] // size
     blocks = total.shape[0] // size
 
+    start = lax.axis_index("col") * width
+
     def fetch(i):
         span = pl.ds(pieces[i], pieces[i + 1] - pieces[i])
         return pltpu.make_async_copy(factor_ref.at[span], held.at[span], arrived.at[i])
@@ -43,13 +45,13 @@
 
     def add(k, carry):
         row = pl.ds(pl.multiple_of(rows_ref[0, k] * size, size), size)
-        col = pl.ds(pl.multiple_of(lax.rem(cols_ref[0, k], width) * size, size), size)
+        col = pl.ds(pl.multiple_of((cols_ref[0, k] - start) * size, size), size)
         total[row, col] += held[k]
         return carry
 
     for i in range(len(pieces) - 1):
         fetch(i).wait()
-        lax.fori_loop(pieces[i], pieces[i + 1], add, 0)
+        lax.fori_loop(pieces[i], pieces[i + 1], add, 0, unroll=2)
 
 
 def merge(factor, rows, cols, row_tiles, col_tiles):
@@ -186,7 +188,6 @@
             for dz in range(1, nz):
                 total = total + zin[p, dz]
             bout[p] = total
-            back(p).start()
 
         span = pl.ds(pl.multiple_of(p * wide, wide), wide)
         for t in range(per):
@@ -215,6 +216,10 @@
             result = chunk(0, dz)
             for t in range(per):
                 own[p, dz, t] = result[:, t * size:(t + 1) * size]
+
+        @pl.when(g > 0)
+        def _():
+            back(p).start()
 
     def second(p):
         for dz in order:

time: 52.4 us -> 52.3 us (level)
  no operation moved by 1% of the time
where the time goes in v9:
time: 52.3 us; the launch traced here: 52.2 us
  Pallas kernels  50.2 us (96%)
  local copies, waits for them, and re-layouts  1.32 us (3%)
  between operations  0.68 us (1%)
    pallas_call x1, Pallas kernels, local(): pl.pallas_call(functools.partial(chain_kernel, groups, nx, nz, panels), o...  46.4 us
    pallas_call x1, Pallas kernels, merge(): pl.pallas_call(functools.partial(merge_kernel, pieces), out_shape=pltpu.V...  3.79 us
    unnamed x6, local copies, waits for them, and re-layouts  1.32 us

profile of v9, /device:TPU:5, one launch (start us, length us, event | category | flops | bytes accessed | tf_op | source)
XLA Modules:
  0.0 52.2 jit_solution(7168729455066257386)
XLA Ops:
  0.6 0.0 copy-start
  0.6 0.0 copy-start.1
  0.7 3.8 %shard_map.68.full_ref = f32[4096,512]{1,0:T(8,128)S(1)} custom-call(s32[1,94]{1,0:T(1,128)} %rows_ref.1, s32[1,94]{1,0:T(1,128)} %cols_ref.1, f32[94,128,128]{2,1,0:T(8,128)} %bitcast.9), custom_call_target="tpu_custom_call" | custom-call | tf_op jit(solution)/shard_map/pallas_call | solution.py:63
  4.5 0.0 copy-done
  4.5 0.0 copy-done.1
  4.5 46.4 %shard_map.69 = (f32[4,64,128]{2,1,0:T(8,128)S(1)}, f32[4,64,128]{2,1,0:T(8,128)S(1)}) custom-call(f32[4,64,128]{2,1,0:T(8,128)S(1)} %bitcast.6, f32[4,128,128]{2,1,0:T(8,128)S(1)} %bitcast.5, f32[4096,512]{1,0:T(8,128)S(1)} %shard_map.68.full_ref), custom_call_target="tpu_custom_call" | custom-call | tf_op jit(solution)/shard_map/pallas_call | solution.py:293
  50.9 0.7 %copy.9 = f32[1,4,64,128]{3,2,1,0:T(8,128)} copy(f32[1,4,64,128]{3,2,1,0:T(8,128)S(1)} %bitcast.8) | data formatting | bytes 262144
  51.5 0.7 %copy.10 = f32[1,4,64,128]{3,2,1,0:T(8,128)} copy(f32[1,4,64,128]{3,2,1,0:T(8,128)S(1)} %bitcast.7) | data formatting | bytes 262144
Async XLA Ops:
  0.6 3.8 %copy-start = (f32[1,4,128,128]{3,2,1,0:T(8,128)S(1)}, f32[1,4,128,128]{3,2,1,0:T(8,128)}, u32[]{:S(2)}) copy-start(f32[1,4,128,128]{3,2,1,0:T(8,128)} %param.6) | copy-start | bytes 786436
  0.6 3.8 %copy-start.1 = (f32[1,4,64,128]{3,2,1,0:T(8,128)S(1)}, f32[1,4,64,128]{3,2,1,0:T(8,128)}, u32[]{:S(2)}) copy-start(f32[1,4,64,128]{3,2,1,0:T(8,128)} %param.5) | copy-start | bytes 393220
